TPU v7x, 32 devices: a whole 2x2x4 slice. The times are simulated.
32 devices in a mesh: groups: 2 (over x), crate: 16 (over z, y, core).
Axes of the slice: x: 2, y: 2, z: 4, core: 2. Of those that a mesh axis runs over, the one named last changes fastest.
Arguments:
- voltages: bfloat16 [4096, 17920], P(('groups', 'crate')), parts along dimension 0, may hold values from -6 to 6
- gains: float32 [256, 2, 2048], P('crate'), may hold values from -4 to 4
- positions: float32 [3, 2048], replicated, may hold values from -64 to 64
- directions: float32 [3, 512], replicated, may hold values from -0.5 to 0.5
- input_order: int32 [2048], replicated, may hold values from 0 to 2047, each once
- delays: int32 [1024, 256], replicated, may hold values from 0 to 31
- search_beams: int32 [16], replicated, may hold values from 0 to 511, as said below
Outputs:
- beam_power: float32 [512, 512, 32], P(('groups', 'crate')), parts along dimension 0
- dm_plane: float32 [2048, 16, 32], P(('groups', 'crate')), parts along dimension 0
There are 2 independent parts, one for each index of `groups`. A program takes and returns all parts, laid end to end along the dimension named above; an argument that names none is the same for every part. Nothing has to cross between parts.
Inputs may be any that keep to these rules, and one draw needn't show every extreme that they name: `input_order`: each antenna is carried by exactly one input row. `search_beams`: 16 distinct beams, among them beam 0 and beam 512 - 1.
All inputs are finite; a program needn't handle non-finite values.
Results may differ from a plain program's by a relative error of at most 0.0082.
Values may be sent and summed in bfloat16 or wider, within the bound.
A program may use at most 64 MiB of HBM per device.

v0:
```python
import math

import jax
import jax.numpy as jnp
from jax import lax
from jax.sharding import PartitionSpec as P

INPUTS = 2048
CH = 256
BEAMS = 512
TRIALS = 1024
TAPS = 4
TIME = 32
SEARCH = 16
FFTLEN = 512


TWO_PI = 2.0 * math.pi


def pfb_window():
    window_len = TAPS * FFTLEN
    sample_index = jnp.arange(window_len, dtype=jnp.int32).astype(jnp.float32)
    offsets = (sample_index - 0.5 * window_len + 0.5) / FFTLEN
    tapering = 0.54 - 0.46 * jnp.cos(TWO_PI * sample_index / (window_len - 1))
    return (jnp.sinc(offsets) * tapering).reshape(TAPS, FFTLEN)


def fold_frames(voltages, window):
    frames = voltages.reshape(voltages.shape[0], TIME + TAPS - 1, FFTLEN)
    summed = window[0] * frames[:, 0:TIME].astype(jnp.float32)
    for tap_index in range(1, TAPS):
        summed = summed + window[tap_index] * frames[:, tap_index : tap_index + TIME].astype(
            jnp.float32
        )
    return summed.astype(jnp.bfloat16)


def dft_table():
    channel_ids = jnp.arange(CH, dtype=jnp.int32)[:, None]
    sample_ids = jnp.arange(FFTLEN, dtype=jnp.int32)[None, :]
    angles = TWO_PI * (channel_ids * sample_ids % FFTLEN).astype(jnp.float32) / FFTLEN
    factor = 1.0 / math.sqrt(FFTLEN)
    stacked = jnp.stack([jnp.cos(angles) * factor, -jnp.sin(angles) * factor], axis=1)
    return stacked.reshape(2 * CH, FFTLEN).astype(jnp.bfloat16)


def time_table():
    step_ids = jnp.arange(TIME, dtype=jnp.int32)[:, None]
    bin_ids = jnp.arange(1, TIME // 2 + 1, dtype=jnp.int32)[None, :]
    angles = TWO_PI * (step_ids * bin_ids % TIME).astype(jnp.float32) / TIME
    factor = 1.0 / math.sqrt(TIME)
    return jnp.concatenate([jnp.cos(angles) * factor, -jnp.sin(angles) * factor], axis=1)


def array_geometry(positions, directions, input_order):
    placed = jnp.take(positions, input_order, axis=1)
    geometry = directions[0][:, None] * placed[0][None, :]
    geometry = geometry + directions[1][:, None] * placed[1][None, :]
    return geometry + directions[2][:, None] * placed[2][None, :]


def steering(geometry, gain_row, frequency):
    phases = TWO_PI * frequency * geometry
    cosine = jnp.cos(phases)
    sine_part = jnp.sin(phases)
    weight_norm = 1.0 / math.sqrt(INPUTS)
    w_real = ((gain_row[0] * cosine + gain_row[1] * sine_part) * weight_norm).astype(jnp.bfloat16)
    w_imag = ((gain_row[1] * cosine - gain_row[0] * sine_part) * weight_norm).astype(jnp.bfloat16)
    upper_rows = jnp.concatenate([w_real, -w_imag], axis=1)
    lower_rows = jnp.concatenate([w_imag, w_real], axis=1)
    return jnp.concatenate([upper_rows, lower_rows], axis=0)


def dedisperse(spectrum, delay_part):
    half_bins = TIME // 2
    bin_ids = jnp.arange(1, half_bins + 1, dtype=jnp.int32)
    turn_counts = delay_part[:, :, None] * bin_ids[None, None, :] % TIME
    angles = TWO_PI * turn_counts.astype(jnp.float32) / TIME
    cosine = jnp.cos(angles)
    sine_part = jnp.sin(angles)
    spec_real = spectrum[:, :, :half_bins]
    spec_imag = spectrum[:, :, half_bins:]
    highest = lax.Precision.HIGHEST
    out_real = jnp.einsum(
        "cbk,dck->dbk", spec_real, cosine, precision=highest, preferred_element_type=jnp.float32
    ) - jnp.einsum(
        "cbk,dck->dbk", spec_imag, sine_part, precision=highest, preferred_element_type=jnp.float32
    )
    out_imag = jnp.einsum(
        "cbk,dck->dbk", spec_real, sine_part, precision=highest, preferred_element_type=jnp.float32
    ) + jnp.einsum(
        "cbk,dck->dbk", spec_imag, cosine, precision=highest, preferred_element_type=jnp.float32
    )
    factor = 1.0 / math.sqrt(CH)
    return jnp.concatenate([out_real, out_imag], axis=2) * factor


def on_device(voltages, gains, positions, directions, input_order, delays, search_beams):
    window = pfb_window()
    folded = fold_frames(voltages, window)
    spectra = jnp.einsum("ks,its->kit", dft_table(), folded, preferred_element_type=jnp.float32)
    spectra = spectra.astype(jnp.bfloat16).reshape(CH, 2, voltages.shape[0], TIME)
    geometry = array_geometry(positions, directions, input_order)
    turned = lax.all_to_all(spectra, "crate", split_axis=0, concat_axis=2, tiled=True)
    local_count = turned.shape[0]
    first_channel = lax.axis_index("crate") * local_count

    def one_channel(packed):
        offsets, channel_data, gain_row = packed
        frequency = 1.0 + (first_channel + offsets).astype(jnp.float32) / CH
        weights = steering(geometry, gain_row, frequency)
        beam_sums = jnp.dot(
            weights,
            channel_data.reshape(2 * INPUTS, channel_data.shape[-1]),
            preferred_element_type=jnp.float32,
        )
        return beam_sums[:BEAMS] * beam_sums[:BEAMS] + beam_sums[BEAMS:] * beam_sums[BEAMS:]

    beam_power = lax.map(one_channel, (jnp.arange(local_count, dtype=jnp.int32), turned, gains))
    local_channels = beam_power.shape[0]
    chosen = jnp.take(beam_power, search_beams, axis=1)
    power_spectra = jnp.dot(
        chosen.reshape(local_channels * SEARCH, TIME),
        time_table(),
        precision=lax.Precision.HIGHEST,
        preferred_element_type=jnp.float32,
    )
    power_spectra = power_spectra.reshape(local_channels, SEARCH, TIME)
    trial_rows = TRIALS // lax.axis_size("crate")
    first_trial = lax.axis_index("crate") * trial_rows
    own_delays = lax.dynamic_slice_in_dim(delays, first_trial, trial_rows, 0)
    dm_plane = dedisperse(lax.all_gather(power_spectra, "crate", axis=0, tiled=True), own_delays)
    return (beam_power, dm_plane)


def solution(mesh):
    in_specs = (P(("groups", "crate"), None), P("crate", None, None), P(), P(), P(), P(), P())
    out_specs = (P(("groups", "crate"), None, None), P(("groups", "crate"), None, None))
    return jax.shard_map(
        on_device, mesh=mesh, in_specs=in_specs, out_specs=out_specs, check_vma=False
    )
```

profile of v0, /device:TPU:0, one launch (start us, length us, event | category | flops | bytes accessed | tf_op | source)
XLA Modules:
  0.0 846.8 jit_solution(9826374699885314655)
XLA Ops:
  3.7 6.5 copy.54
  10.3 8.5 %fusion.36 = bf16[512,128,32]{1,0,2:T(8,128)(2,1)S(1)} fusion(bf16[512,512,1]{1,0,2:T(8,128)(2,1)S(1)} %reshape.161, bf16[128,35,512]{0,2,1:T(8,128)(2,1)} %bitcast.48, f32[512]{0:T(512)S(1)} %get-tuple-element.119, f32[512]{0:T(512)S(1)} %get-tuple-element.120, f32[512]{0:T(512)S(1)} %get-tuple-element.121, f32[512]{0:T(512)S(1)} %get-tuple-element.118), kind=kOutput, calls=%fused_computation.44 | convolution fusion | flops 2174746624 | bytes 21504000 | tf_op jit(solution)/shard_map/ks,its->kit/dot_general | solution.py:102
  18.8 6.8 copy.56
  25.5 7.6 all-to-all-start
  33.5 5.5 gather_fusion
  41.1 69.7 %all-to-all-done = bf16[256,2,128,32]{2,1,3,0:T(2,128)(2,1)} async-done(((bf16[256,2,128,32]{2,1,3,0:T(2,128)(2,1)}), bf16[256,2,128,32]{2,1,3,0:T(2,128)(2,1)}, u32[]{:S(2)}, u32[]{:S(2)}) %all-to-all-start) | async-done | bytes 4194336 | tf_op jit(solution)/shard_map/all_to_all | solution.py:105
  110.8 18.8 %copy.57 = bf16[16,2,16,128,32]{4,3,2,1,0:T(8,128)(2,1)} copy(bf16[16,2,16,128,32]{3,1,4,0,2:T(2,128)(2,1)} %bitcast.3) | data formatting | bytes 8388608 | tf_op jit(solution)/shard_map/all_to_all | solution.py:105
  129.6 635.4 %while.11 = (s32[]{:T(128)}, f32[16,512,32]{1,2,0:T(8,128)S(1)}, f32[16,2,2048]{2,1,0:T(2,128)}, s32[16]{0:T(128)S(1)}, s32[]{:T(128)}, /*index=5*/bf16[16,2,204...) while((s32[]{:T(128)}, f32[16,512,32]{1,2,0:T(8,128)S(1)}, ...), condition=%wide.region_1.2_spmd.clone, body=%wide.region_0.1_spmd.clone.sunk | while | flops 333496320 | bytes 13824269 | solution.py:120
  131.8 17.2 %fusion.114 = (bf16[512,2048]{1,0:T(8,128)(2,1)S(1)}, bf16[512,2048]{1,0:T(8,128)(2,1)S(1)}) fusion(f32[2048]{0:T(1024)S(1)} %get-tuple-element.253, f32[512]{0:T(512)S(1)} %get-tuple-element.254, f32[2048]{0:T(1024)S(1)} %get-tuple-element.251, f32[512]{0:T(512)S(1)} %get-tuple-element.252, f32[2048]{0:T(1024)S(1)} %get-tuple-element.249, ...), kind=kLoop, calls=%fused_computation.23.clone.2 | loop fusion | flops 16777216 | bytes 4241412 | tf_op jit(solution)/shard_map/while/body/eval_jaxpr/convert_element_type | solution.py:69
  148.9 16.6 %fusion.115 = bf16[512,2048]{1,0:T(8,128)(2,1)S(1)} fusion(f32[2048]{0:T(1024)S(1)} %bitcast.51, f32[2048]{0:T(1024)S(1)} %get-tuple-element.253, f32[512]{0:T(512)S(1)} %get-tuple-element.254, f32[2048]{0:T(1024)S(1)} %get-tuple-element.251, f32[512]{0:T(512)S(1)} %get-tuple-element.252, f32[2048]{0:T(1024)S(1)} %get-tuple-element.249, ...), kind=kLoop, calls=%fused_computation.33.clone.1 | loop fusion | flops 14680064 | bytes 2144260 | tf_op jit(solution)/shard_map/while/body/eval_jaxpr/neg | solution.py:70
  171.5 17.2 %fusion.114 = (bf16[512,2048]{1,0:T(8,128)(2,1)S(1)}, bf16[512,2048]{1,0:T(8,128)(2,1)S(1)}) fusion(f32[2048]{0:T(1024)S(1)} %get-tuple-element.253, f32[512]{0:T(512)S(1)} %get-tuple-element.254, f32[2048]{0:T(1024)S(1)} %get-tuple-element.251, f32[512]{0:T(512)S(1)} %get-tuple-element.252, f32[2048]{0:T(1024)S(1)} %get-tuple-element.249, ...), kind=kLoop, calls=%fused_computation.23.clone.2 | loop fusion | flops 16777216 | bytes 4241412 | tf_op jit(solution)/shard_map/while/body/eval_jaxpr/convert_element_type | solution.py:69
  188.7 16.6 %fusion.115 = bf16[512,2048]{1,0:T(8,128)(2,1)S(1)} fusion(f32[2048]{0:T(1024)S(1)} %bitcast.51, f32[2048]{0:T(1024)S(1)} %get-tuple-element.253, f32[512]{0:T(512)S(1)} %get-tuple-element.254, f32[2048]{0:T(1024)S(1)} %get-tuple-element.251, f32[512]{0:T(512)S(1)} %get-tuple-element.252, f32[2048]{0:T(1024)S(1)} %get-tuple-element.249, ...), kind=kLoop, calls=%fused_computation.33.clone.1 | loop fusion | flops 14680064 | bytes 2144260 | tf_op jit(solution)/shard_map/while/body/eval_jaxpr/neg | solution.py:70
  211.2 17.2 %fusion.114 = (bf16[512,2048]{1,0:T(8,128)(2,1)S(1)}, bf16[512,2048]{1,0:T(8,128)(2,1)S(1)}) fusion(f32[2048]{0:T(1024)S(1)} %get-tuple-element.253, f32[512]{0:T(512)S(1)} %get-tuple-element.254, f32[2048]{0:T(1024)S(1)} %get-tuple-element.251, f32[512]{0:T(512)S(1)} %get-tuple-element.252, f32[2048]{0:T(1024)S(1)} %get-tuple-element.249, ...), kind=kLoop, calls=%fused_computation.23.clone.2 | loop fusion | flops 16777216 | bytes 4241412 | tf_op jit(solution)/shard_map/while/body/eval_jaxpr/convert_element_type | solution.py:69
  228.4 16.6 %fusion.115 = bf16[512,2048]{1,0:T(8,128)(2,1)S(1)} fusion(f32[2048]{0:T(1024)S(1)} %bitcast.51, f32[2048]{0:T(1024)S(1)} %get-tuple-element.253, f32[512]{0:T(512)S(1)} %get-tuple-element.254, f32[2048]{0:T(1024)S(1)} %get-tuple-element.251, f32[512]{0:T(512)S(1)} %get-tuple-element.252, f32[2048]{0:T(1024)S(1)} %get-tuple-element.249, ...), kind=kLoop, calls=%fused_computation.33.clone.1 | loop fusion | flops 14680064 | bytes 2144260 | tf_op jit(solution)/shard_map/while/body/eval_jaxpr/neg | solution.py:70
  250.9 17.2 %fusion.114 = (bf16[512,2048]{1,0:T(8,128)(2,1)S(1)}, bf16[512,2048]{1,0:T(8,128)(2,1)S(1)}) fusion(f32[2048]{0:T(1024)S(1)} %get-tuple-element.253, f32[512]{0:T(512)S(1)} %get-tuple-element.254, f32[2048]{0:T(1024)S(1)} %get-tuple-element.251, f32[512]{0:T(512)S(1)} %get-tuple-element.252, f32[2048]{0:T(1024)S(1)} %get-tuple-element.249, ...), kind=kLoop, calls=%fused_computation.23.clone.2 | loop fusion | flops 16777216 | bytes 4241412 | tf_op jit(solution)/shard_map/while/body/eval_jaxpr/convert_element_type | solution.py:69
  268.1 16.6 %fusion.115 = bf16[512,2048]{1,0:T(8,128)(2,1)S(1)} fusion(f32[2048]{0:T(1024)S(1)} %bitcast.51, f32[2048]{0:T(1024)S(1)} %get-tuple-element.253, f32[512]{0:T(512)S(1)} %get-tuple-element.254, f32[2048]{0:T(1024)S(1)} %get-tuple-element.251, f32[512]{0:T(512)S(1)} %get-tuple-element.252, f32[2048]{0:T(1024)S(1)} %get-tuple-element.249, ...), kind=kLoop, calls=%fused_computation.33.clone.1 | loop fusion | flops 14680064 | bytes 2144260 | tf_op jit(solution)/shard_map/while/body/eval_jaxpr/neg | solution.py:70
  290.6 17.2 %fusion.114 = (bf16[512,2048]{1,0:T(8,128)(2,1)S(1)}, bf16[512,2048]{1,0:T(8,128)(2,1)S(1)}) fusion(f32[2048]{0:T(1024)S(1)} %get-tuple-element.253, f32[512]{0:T(512)S(1)} %get-tuple-element.254, f32[2048]{0:T(1024)S(1)} %get-tuple-element.251, f32[512]{0:T(512)S(1)} %get-tuple-element.252, f32[2048]{0:T(1024)S(1)} %get-tuple-element.249, ...), kind=kLoop, calls=%fused_computation.23.clone.2 | loop fusion | flops 16777216 | bytes 4241412 | tf_op jit(solution)/shard_map/while/body/eval_jaxpr/convert_element_type | solution.py:69
  307.8 16.6 %fusion.115 = bf16[512,2048]{1,0:T(8,128)(2,1)S(1)} fusion(f32[2048]{0:T(1024)S(1)} %bitcast.51, f32[2048]{0:T(1024)S(1)} %get-tuple-element.253, f32[512]{0:T(512)S(1)} %get-tuple-element.254, f32[2048]{0:T(1024)S(1)} %get-tuple-element.251, f32[512]{0:T(512)S(1)} %get-tuple-element.252, f32[2048]{0:T(1024)S(1)} %get-tuple-element.249, ...), kind=kLoop, calls=%fused_computation.33.clone.1 | loop fusion | flops 14680064 | bytes 2144260 | tf_op jit(solution)/shard_map/while/body/eval_jaxpr/neg | solution.py:70
  330.3 17.2 %fusion.114 = (bf16[512,2048]{1,0:T(8,128)(2,1)S(1)}, bf16[512,2048]{1,0:T(8,128)(2,1)S(1)}) fusion(f32[2048]{0:T(1024)S(1)} %get-tuple-element.253, f32[512]{0:T(512)S(1)} %get-tuple-element.254, f32[2048]{0:T(1024)S(1)} %get-tuple-element.251, f32[512]{0:T(512)S(1)} %get-tuple-element.252, f32[2048]{0:T(1024)S(1)} %get-tuple-element.249, ...), kind=kLoop, calls=%fused_computation.23.clone.2 | loop fusion | flops 16777216 | bytes 4241412 | tf_op jit(solution)/shard_map/while/body/eval_jaxpr/convert_element_type | solution.py:69
  347.5 16.6 %fusion.115 = bf16[512,2048]{1,0:T(8,128)(2,1)S(1)} fusion(f32[2048]{0:T(1024)S(1)} %bitcast.51, f32[2048]{0:T(1024)S(1)} %get-tuple-element.253, f32[512]{0:T(512)S(1)} %get-tuple-element.254, f32[2048]{0:T(1024)S(1)} %get-tuple-element.251, f32[512]{0:T(512)S(1)} %get-tuple-element.252, f32[2048]{0:T(1024)S(1)} %get-tuple-element.249, ...), kind=kLoop, calls=%fused_computation.33.clone.1 | loop fusion | flops 14680064 | bytes 2144260 | tf_op jit(solution)/shard_map/while/body/eval_jaxpr/neg | solution.py:70
  370.0 17.2 %fusion.114 = (bf16[512,2048]{1,0:T(8,128)(2,1)S(1)}, bf16[512,2048]{1,0:T(8,128)(2,1)S(1)}) fusion(f32[2048]{0:T(1024)S(1)} %get-tuple-element.253, f32[512]{0:T(512)S(1)} %get-tuple-element.254, f32[2048]{0:T(1024)S(1)} %get-tuple-element.251, f32[512]{0:T(512)S(1)} %get-tuple-element.252, f32[2048]{0:T(1024)S(1)} %get-tuple-element.249, ...), kind=kLoop, calls=%fused_computation.23.clone.2 | loop fusion | flops 16777216 | bytes 4241412 | tf_op jit(solution)/shard_map/while/body/eval_jaxpr/convert_element_type | solution.py:69
  387.2 16.6 %fusion.115 = bf16[512,2048]{1,0:T(8,128)(2,1)S(1)} fusion(f32[2048]{0:T(1024)S(1)} %bitcast.51, f32[2048]{0:T(1024)S(1)} %get-tuple-element.253, f32[512]{0:T(512)S(1)} %get-tuple-element.254, f32[2048]{0:T(1024)S(1)} %get-tuple-element.251, f32[512]{0:T(512)S(1)} %get-tuple-element.252, f32[2048]{0:T(1024)S(1)} %get-tuple-element.249, ...), kind=kLoop, calls=%fused_computation.33.clone.1 | loop fusion | flops 14680064 | bytes 2144260 | tf_op jit(solution)/shard_map/while/body/eval_jaxpr/neg | solution.py:70
  409.7 17.2 %fusion.114 = (bf16[512,2048]{1,0:T(8,128)(2,1)S(1)}, bf16[512,2048]{1,0:T(8,128)(2,1)S(1)}) fusion(f32[2048]{0:T(1024)S(1)} %get-tuple-element.253, f32[512]{0:T(512)S(1)} %get-tuple-element.254, f32[2048]{0:T(1024)S(1)} %get-tuple-element.251, f32[512]{0:T(512)S(1)} %get-tuple-element.252, f32[2048]{0:T(1024)S(1)} %get-tuple-element.249, ...), kind=kLoop, calls=%fused_computation.23.clone.2 | loop fusion | flops 16777216 | bytes 4241412 | tf_op jit(solution)/shard_map/while/body/eval_jaxpr/convert_element_type | solution.py:69
  426.9 16.6 %fusion.115 = bf16[512,2048]{1,0:T(8,128)(2,1)S(1)} fusion(f32[2048]{0:T(1024)S(1)} %bitcast.51, f32[2048]{0:T(1024)S(1)} %get-tuple-element.253, f32[512]{0:T(512)S(1)} %get-tuple-element.254, f32[2048]{0:T(1024)S(1)} %get-tuple-element.251, f32[512]{0:T(512)S(1)} %get-tuple-element.252, f32[2048]{0:T(1024)S(1)} %get-tuple-element.249, ...), kind=kLoop, calls=%fused_computation.33.clone.1 | loop fusion | flops 14680064 | bytes 2144260 | tf_op jit(solution)/shard_map/while/body/eval_jaxpr/neg | solution.py:70
  449.4 17.2 %fusion.114 = (bf16[512,2048]{1,0:T(8,128)(2,1)S(1)}, bf16[512,2048]{1,0:T(8,128)(2,1)S(1)}) fusion(f32[2048]{0:T(1024)S(1)} %get-tuple-element.253, f32[512]{0:T(512)S(1)} %get-tuple-element.254, f32[2048]{0:T(1024)S(1)} %get-tuple-element.251, f32[512]{0:T(512)S(1)} %get-tuple-element.252, f32[2048]{0:T(1024)S(1)} %get-tuple-element.249, ...), kind=kLoop, calls=%fused_computation.23.clone.2 | loop fusion | flops 16777216 | bytes 4241412 | tf_op jit(solution)/shard_map/while/body/eval_jaxpr/convert_element_type | solution.py:69
  466.6 16.6 %fusion.115 = bf16[512,2048]{1,0:T(8,128)(2,1)S(1)} fusion(f32[2048]{0:T(1024)S(1)} %bitcast.51, f32[2048]{0:T(1024)S(1)} %get-tuple-element.253, f32[512]{0:T(512)S(1)} %get-tuple-element.254, f32[2048]{0:T(1024)S(1)} %get-tuple-element.251, f32[512]{0:T(512)S(1)} %get-tuple-element.252, f32[2048]{0:T(1024)S(1)} %get-tuple-element.249, ...), kind=kLoop, calls=%fused_computation.33.clone.1 | loop fusion | flops 14680064 | bytes 2144260 | tf_op jit(solution)/shard_map/while/body/eval_jaxpr/neg | solution.py:70
  489.1 17.2 %fusion.114 = (bf16[512,2048]{1,0:T(8,128)(2,1)S(1)}, bf16[512,2048]{1,0:T(8,128)(2,1)S(1)}) fusion(f32[2048]{0:T(1024)S(1)} %get-tuple-element.253, f32[512]{0:T(512)S(1)} %get-tuple-element.254, f32[2048]{0:T(1024)S(1)} %get-tuple-element.251, f32[512]{0:T(512)S(1)} %get-tuple-element.252, f32[2048]{0:T(1024)S(1)} %get-tuple-element.249, ...), kind=kLoop, calls=%fused_computation.23.clone.2 | loop fusion | flops 16777216 | bytes 4241412 | tf_op jit(solution)/shard_map/while/body/eval_jaxpr/convert_element_type | solution.py:69
  506.3 16.6 %fusion.115 = bf16[512,2048]{1,0:T(8,128)(2,1)S(1)} fusion(f32[2048]{0:T(1024)S(1)} %bitcast.51, f32[2048]{0:T(1024)S(1)} %get-tuple-element.253, f32[512]{0:T(512)S(1)} %get-tuple-element.254, f32[2048]{0:T(1024)S(1)} %get-tuple-element.251, f32[512]{0:T(512)S(1)} %get-tuple-element.252, f32[2048]{0:T(1024)S(1)} %get-tuple-element.249, ...), kind=kLoop, calls=%fused_computation.33.clone.1 | loop fusion | flops 14680064 | bytes 2144260 | tf_op jit(solution)/shard_map/while/body/eval_jaxpr/neg | solution.py:70
  528.8 17.2 %fusion.114 = (bf16[512,2048]{1,0:T(8,128)(2,1)S(1)}, bf16[512,2048]{1,0:T(8,128)(2,1)S(1)}) fusion(f32[2048]{0:T(1024)S(1)} %get-tuple-element.253, f32[512]{0:T(512)S(1)} %get-tuple-element.254, f32[2048]{0:T(1024)S(1)} %get-tuple-element.251, f32[512]{0:T(512)S(1)} %get-tuple-element.252, f32[2048]{0:T(1024)S(1)} %get-tuple-element.249, ...), kind=kLoop, calls=%fused_computation.23.clone.2 | loop fusion | flops 16777216 | bytes 4241412 | tf_op jit(solution)/shard_map/while/body/eval_jaxpr/convert_element_type | solution.py:69
  546.0 16.6 %fusion.115 = bf16[512,2048]{1,0:T(8,128)(2,1)S(1)} fusion(f32[2048]{0:T(1024)S(1)} %bitcast.51, f32[2048]{0:T(1024)S(1)} %get-tuple-element.253, f32[512]{0:T(512)S(1)} %get-tuple-element.254, f32[2048]{0:T(1024)S(1)} %get-tuple-element.251, f32[512]{0:T(512)S(1)} %get-tuple-element.252, f32[2048]{0:T(1024)S(1)} %get-tuple-element.249, ...), kind=kLoop, calls=%fused_computation.33.clone.1 | loop fusion | flops 14680064 | bytes 2144260 | tf_op jit(solution)/shard_map/while/body/eval_jaxpr/neg | solution.py:70
  568.5 17.2 %fusion.114 = (bf16[512,2048]{1,0:T(8,128)(2,1)S(1)}, bf16[512,2048]{1,0:T(8,128)(2,1)S(1)}) fusion(f32[2048]{0:T(1024)S(1)} %get-tuple-element.253, f32[512]{0:T(512)S(1)} %get-tuple-element.254, f32[2048]{0:T(1024)S(1)} %get-tuple-element.251, f32[512]{0:T(512)S(1)} %get-tuple-element.252, f32[2048]{0:T(1024)S(1)} %get-tuple-element.249, ...), kind=kLoop, calls=%fused_computation.23.clone.2 | loop fusion | flops 16777216 | bytes 4241412 | tf_op jit(solution)/shard_map/while/body/eval_jaxpr/convert_element_type | solution.py:69
  585.7 16.6 %fusion.115 = bf16[512,2048]{1,0:T(8,128)(2,1)S(1)} fusion(f32[2048]{0:T(1024)S(1)} %bitcast.51, f32[2048]{0:T(1024)S(1)} %get-tuple-element.253, f32[512]{0:T(512)S(1)} %get-tuple-element.254, f32[2048]{0:T(1024)S(1)} %get-tuple-element.251, f32[512]{0:T(512)S(1)} %get-tuple-element.252, f32[2048]{0:T(1024)S(1)} %get-tuple-element.249, ...), kind=kLoop, calls=%fused_computation.33.clone.1 | loop fusion | flops 14680064 | bytes 2144260 | tf_op jit(solution)/shard_map/while/body/eval_jaxpr/neg | solution.py:70
  608.2 17.2 %fusion.114 = (bf16[512,2048]{1,0:T(8,128)(2,1)S(1)}, bf16[512,2048]{1,0:T(8,128)(2,1)S(1)}) fusion(f32[2048]{0:T(1024)S(1)} %get-tuple-element.253, f32[512]{0:T(512)S(1)} %get-tuple-element.254, f32[2048]{0:T(1024)S(1)} %get-tuple-element.251, f32[512]{0:T(512)S(1)} %get-tuple-element.252, f32[2048]{0:T(1024)S(1)} %get-tuple-element.249, ...), kind=kLoop, calls=%fused_computation.23.clone.2 | loop fusion | flops 16777216 | bytes 4241412 | tf_op jit(solution)/shard_map/while/body/eval_jaxpr/convert_element_type | solution.py:69
  625.4 16.6 %fusion.115 = bf16[512,2048]{1,0:T(8,128)(2,1)S(1)} fusion(f32[2048]{0:T(1024)S(1)} %bitcast.51, f32[2048]{0:T(1024)S(1)} %get-tuple-element.253, f32[512]{0:T(512)S(1)} %get-tuple-element.254, f32[2048]{0:T(1024)S(1)} %get-tuple-element.251, f32[512]{0:T(512)S(1)} %get-tuple-element.252, f32[2048]{0:T(1024)S(1)} %get-tuple-element.249, ...), kind=kLoop, calls=%fused_computation.33.clone.1 | loop fusion | flops 14680064 | bytes 2144260 | tf_op jit(solution)/shard_map/while/body/eval_jaxpr/neg | solution.py:70
  648.0 17.2 %fusion.114 = (bf16[512,2048]{1,0:T(8,128)(2,1)S(1)}, bf16[512,2048]{1,0:T(8,128)(2,1)S(1)}) fusion(f32[2048]{0:T(1024)S(1)} %get-tuple-element.253, f32[512]{0:T(512)S(1)} %get-tuple-element.254, f32[2048]{0:T(1024)S(1)} %get-tuple-element.251, f32[512]{0:T(512)S(1)} %get-tuple-element.252, f32[2048]{0:T(1024)S(1)} %get-tuple-element.249, ...), kind=kLoop, calls=%fused_computation.23.clone.2 | loop fusion | flops 16777216 | bytes 4241412 | tf_op jit(solution)/shard_map/while/body/eval_jaxpr/convert_element_type | solution.py:69
  665.1 16.6 %fusion.115 = bf16[512,2048]{1,0:T(8,128)(2,1)S(1)} fusion(f32[2048]{0:T(1024)S(1)} %bitcast.51, f32[2048]{0:T(1024)S(1)} %get-tuple-element.253, f32[512]{0:T(512)S(1)} %get-tuple-element.254, f32[2048]{0:T(1024)S(1)} %get-tuple-element.251, f32[512]{0:T(512)S(1)} %get-tuple-element.252, f32[2048]{0:T(1024)S(1)} %get-tuple-element.249, ...), kind=kLoop, calls=%fused_computation.33.clone.1 | loop fusion | flops 14680064 | bytes 2144260 | tf_op jit(solution)/shard_map/while/body/eval_jaxpr/neg | solution.py:70
  687.7 17.2 %fusion.114 = (bf16[512,2048]{1,0:T(8,128)(2,1)S(1)}, bf16[512,2048]{1,0:T(8,128)(2,1)S(1)}) fusion(f32[2048]{0:T(1024)S(1)} %get-tuple-element.253, f32[512]{0:T(512)S(1)} %get-tuple-element.254, f32[2048]{0:T(1024)S(1)} %get-tuple-element.251, f32[512]{0:T(512)S(1)} %get-tuple-element.252, f32[2048]{0:T(1024)S(1)} %get-tuple-element.249, ...), kind=kLoop, calls=%fused_computation.23.clone.2 | loop fusion | flops 16777216 | bytes 4241412 | tf_op jit(solution)/shard_map/while/body/eval_jaxpr/convert_element_type | solution.py:69
  704.8 16.6 %fusion.115 = bf16[512,2048]{1,0:T(8,128)(2,1)S(1)} fusion(f32[2048]{0:T(1024)S(1)} %bitcast.51, f32[2048]{0:T(1024)S(1)} %get-tuple-element.253, f32[512]{0:T(512)S(1)} %get-tuple-element.254, f32[2048]{0:T(1024)S(1)} %get-tuple-element.251, f32[512]{0:T(512)S(1)} %get-tuple-element.252, f32[2048]{0:T(1024)S(1)} %get-tuple-element.249, ...), kind=kLoop, calls=%fused_computation.33.clone.1 | loop fusion | flops 14680064 | bytes 2144260 | tf_op jit(solution)/shard_map/while/body/eval_jaxpr/neg | solution.py:70
  727.4 17.2 %fusion.114 = (bf16[512,2048]{1,0:T(8,128)(2,1)S(1)}, bf16[512,2048]{1,0:T(8,128)(2,1)S(1)}) fusion(f32[2048]{0:T(1024)S(1)} %get-tuple-element.253, f32[512]{0:T(512)S(1)} %get-tuple-element.254, f32[2048]{0:T(1024)S(1)} %get-tuple-element.251, f32[512]{0:T(512)S(1)} %get-tuple-element.252, f32[2048]{0:T(1024)S(1)} %get-tuple-element.249, ...), kind=kLoop, calls=%fused_computation.23.clone.2 | loop fusion | flops 16777216 | bytes 4241412 | tf_op jit(solution)/shard_map/while/body/eval_jaxpr/convert_element_type | solution.py:69
  744.5 16.6 %fusion.115 = bf16[512,2048]{1,0:T(8,128)(2,1)S(1)} fusion(f32[2048]{0:T(1024)S(1)} %bitcast.51, f32[2048]{0:T(1024)S(1)} %get-tuple-element.253, f32[512]{0:T(512)S(1)} %get-tuple-element.254, f32[2048]{0:T(1024)S(1)} %get-tuple-element.251, f32[512]{0:T(512)S(1)} %get-tuple-element.252, f32[2048]{0:T(1024)S(1)} %get-tuple-element.249, ...), kind=kLoop, calls=%fused_computation.33.clone.1 | loop fusion | flops 14680064 | bytes 2144260 | tf_op jit(solution)/shard_map/while/body/eval_jaxpr/neg | solution.py:70
  765.0 3.7 copy.59
  768.7 2.7 gather_fusion.1
  771.8 45.4 %all_gather.3 = f32[256,16,32]{2,1,0:T(8,128)S(1)} all-gather(f32[16,16,32]{2,1,0:T(8,128)S(1)} %fusion.56), channel_id=1, replica_groups=mesh['groups'=2,'crate'=16] {'crate'}, dimensions={0}, use_global_device_ids=true | all-gather | bytes 557056 | tf_op jit(solution)/shard_map/all_gather | solution.py:133
  819.2 2.6 copy.68
  821.8 5.7 fusion.48
  827.5 5.7 fusion.50
  834.4 6.2 fusion.38
  840.7 4.9 fusion.37
  (122 shorter events, 93.7 us)
Async XLA Ops:
  0.6 38.4 %copy-start = (s32[1024,256]{1,0:T(8,128)S(1)}, s32[1024,256]{1,0:T(8,128)}, u32[]{:S(2)}) copy-start(s32[1024,256]{1,0:T(8,128)} %param.14) | copy-start | bytes 3145732
  25.5 7.6 copy-start.3
  25.5 8.0 copy-start.4
  25.5 13.5 %copy-start.6 = (s32[16]{0:T(128)S(1)}, s32[16]{0:T(128)}, u32[]{:S(2)}) copy-start(s32[16]{0:T(128)} %param.15) | copy-start | bytes 196
  25.5 85.2 %all-to-all-start = ((bf16[256,2,128,32]{2,1,3,0:T(2,128)(2,1)}), bf16[256,2,128,32]{2,1,3,0:T(2,128)(2,1)}, u32[]{:S(2)}, u32[]{:S(2)}) async-start(bf16[256,2,128,32]{2,1,3,0:T(2,128)(2,1)} %copy.56), calls=%async_computation | async-start | bytes 8388608 | tf_op jit(solution)/shard_map/all_to_all | solution.py:105
  33.1 7.8 copy-start.5
  110.8 18.8 %copy-start.1 = (f32[16,512,32]{1,2,0:T(8,128)S(1)}, f32[16,512,32]{1,2,0:T(8,128)}, u32[]{:S(2)}) copy-start(f32[16,512,32]{1,2,0:T(8,128)} %custom-call.4) | copy-start | bytes 3145732
  765.0 6.8 copy-start.2
  834.4 6.3 copy-start.7
where the time goes:
time: 857 us; the launch traced here: 847 us
  other arithmetic  544 us (63%)
  local copies, waits for them, and re-layouts  96.2 us (11%)
  matrix products  71.6 us (8%)
  waiting for transfers between devices  69.7 us (8%)
  blocking collectives  45.4 us (5%)
  loops' own time  11.3 us (1%)
    convert_element_type x16, other arithmetic, steering(): ((gain_row[1] * cosine - gain_row[0] * sine_part) * weight_norm).astype(j...  275 us
    neg x16, other arithmetic, steering(): upper_rows = jnp.concatenate([w_real, -w_imag], axis=1)  266 us
    all_to_all x1, waiting for transfers between devices, on_device(): lax.all_to_all(spectra, 'crate', split_axis=0, concat_axis=2, tiled=True)  69.7 us
    all_gather x1, blocking collectives, on_device(): lax.all_gather(power_spectra, 'crate', axis=0, tiled=True)  45.4 us
    dot_general x16, matrix products, one_channel(): jnp.dot(weights, channel_data.reshape(2 * INPUTS, channel_data.shape[-1])...  40.2 us
    dynamic_slice x32, local copies, waits for them, and re-layouts, on_device(): lax.map(one_channel, (jnp.arange(local_count, dtype=jnp.int32), turned, g...  30.2 us
    all_to_all x1, local copies, waits for them, and re-layouts, on_device(): lax.all_to_all(spectra, 'crate', split_axis=0, concat_axis=2, tiled=True)  18.8 us
  transfers between devices with their start and end apart: 1, of which 1 were waited for; matrix products, arithmetic and copies ran while one was open for 1% of the time, Pallas kernels for 0%

commit v1 on v0

--- a/solution.py
+++ b/solution.py
@@ -1,8 +1,12 @@
+import functools
 import math
 
 import jax
 import jax.numpy as jnp
+import numpy as np
 from jax import lax
+from jax.experimental import pallas as pl
+from jax.experimental.pallas import tpu as pltpu
 from jax.sharding import PartitionSpec as P
 
 INPUTS = 2048
@@ -96,7 +100,7 @@
     return jnp.concatenate([out_real, out_imag], axis=2) * factor
 
 
-def on_device(voltages, gains, positions, directions, input_order, delays, search_beams):
+def plain_device(voltages, gains, positions, directions, input_order, delays, search_beams):
     window = pfb_window()
     folded = fold_frames(voltages, window)
     spectra = jnp.einsum("ks,its->kit", dft_table(), folded, preferred_element_type=jnp.float32)
@@ -134,9 +138,313 @@
     return (beam_power, dm_plane)
 
 
+LANES = 128
+MESH = pl.DeviceIdType.MESH
+
+
+def constant_tables():
+    n = np.arange(TAPS * FFTLEN, dtype=np.float64)
+    u = (n - 0.5 * TAPS * FFTLEN + 0.5) / FFTLEN
+    taper = 0.54 - 0.46 * np.cos(TWO_PI * n / (TAPS * FFTLEN - 1))
+    window = (np.sinc(u) * taper).reshape(TAPS, FFTLEN).astype(np.float32)
+    c = np.arange(CH)[:, None]
+    s = np.arange(FFTLEN)[None, :]
+    angles = TWO_PI * (c * s % FFTLEN) / FFTLEN
+    table = np.stack([np.cos(angles), -np.sin(angles)], axis=1) / math.sqrt(FFTLEN)
+    dft = table.reshape(2 * CH, FFTLEN).astype(jnp.bfloat16)
+    t = np.arange(TIME)[:, None]
+    k = np.arange(1, TIME // 2 + 1)[None, :]
+    turns = TWO_PI * (t * k % TIME) / TIME
+    steps = np.concatenate([np.cos(turns), -np.sin(turns)], axis=1) / math.sqrt(TIME * CH)
+    spread = np.repeat(steps, SEARCH, axis=1).astype(np.float32)
+    return window, dft, spread
+
+
+def turn(x):
+    y = (x - jnp.round(x)) * math.pi
+    z = y * y
+    sine = 1.0 / math.factorial(11) * -1.0
+    for power in (9, 7, 5, 3, 1):
+        sine = sine * z + (-1.0) ** (power // 2) / math.factorial(power)
+    sine = sine * y
+    cosine = 1.0 / math.factorial(12)
+    for power in (10, 8, 6, 4, 2, 0):
+        cosine = cosine * z + (-1.0) ** (power // 2) / math.factorial(power)
+    return 1.0 - 2.0 * sine * sine, 2.0 * sine * cosine
+
+
+def split_three(x):
+    high = x.astype(jnp.bfloat16)
+    left = x - high.astype(jnp.float32)
+    middle = left.astype(jnp.bfloat16)
+    return high, middle, (left - middle.astype(jnp.float32)).astype(jnp.bfloat16)
+
+
+def crate_kernel(
+    n, volts, window, dft, gains, positions, directions, order, delays, beams, spread,
+    power, plane,
+    folded, frames, sent, held, parts, wheel, sums, twist, onehot, mine, gathered,
+    send_sem, recv_sem, own_sem, share_send, share_recv,
+):
+    me = lax.axis_index("crate")
+    rows = 2 * CH // n
+    local = CH // n
+    trials = TRIALS // n
+    half = TIME // 2
+    f32, bf16 = jnp.float32, jnp.bfloat16
+
+    def peer(step):
+        return lax.rem(me + step, n)
+
+    barrier = pltpu.get_barrier_semaphore()
+
+    def greet(step, carry):
+        pl.semaphore_signal(barrier, inc=1, device_id={"crate": peer(step)}, device_id_type=MESH)
+        return carry
+
+    lax.fori_loop(1, n, greet, 0)
+
+    def fold(t, carry):
+        total = None
+        for tap in range(TAPS):
+            at = pl.multiple_of((t + tap) * FFTLEN, FFTLEN)
+            term = window[tap : tap + 1, :] * volts[:, pl.ds(at, FFTLEN)].astype(f32)
+            total = term if total is None else total + term
+        folded[t] = total.astype(bf16)
+        return carry
+
+    lax.fori_loop(0, TIME, fold, 0)
+
+    def channelize(pair, carry):
+        block = folded[pl.ds(2 * pair, 2)].reshape(2 * LANES, FFTLEN)
+        out = lax.dot_general(
+            dft[...], block, (((1,), (1,)), ((), ())), preferred_element_type=f32
+        )
+        for which in range(2):
+            at = pl.multiple_of((2 * pair + which) * 2 * CH, 2 * CH)
+            frames[pl.ds(at, 2 * CH), :] = out[:, which * LANES : (which + 1) * LANES]
+        return carry
+
+    lax.fori_loop(0, TIME // 2, channelize, 0)
+
+    def pack(step):
+        first = peer(step) * rows
+        for row in range(rows):
+            sent[step, row] = frames[pl.ds(first + row, TIME, stride=2 * CH), :].astype(bf16)
+
+    def turned(step):
+        return pltpu.make_async_remote_copy(
+            src_ref=sent.at[step],
+            dst_ref=held.at[step],
+            send_sem=send_sem.at[step],
+            recv_sem=recv_sem.at[step],
+            device_id={"crate": peer(step)},
+            device_id_type=MESH,
+        )
+
+    pl.semaphore_wait(barrier, n - 1)
+
+    def send(step, carry):
+        pack(step)
+        turned(step).start()
+        return carry
+
+    lax.fori_loop(1, n, send, 0)
+    pack(0)
+    own = pltpu.make_async_copy(sent.at[0], held.at[0], own_sem)
+    own.start()
+
+    for index, part in enumerate(split_three(positions[...])):
+        parts[index] = part
+    beam_ids = lax.broadcasted_iota(jnp.int32, (BEAMS, TIME * SEARCH), 0)
+    onehot[...] = jnp.where(beam_ids == beams[...], 1.0, 0.0).astype(bf16)
+
+    at = pl.multiple_of(me * trials, trials)
+    cos_one, sin_one = turn(delays[pl.ds(at, trials), :].astype(f32) * (1.0 / TIME))
+    cosine, sine = cos_one, sin_one
+    for k in range(half):
+        low = cosine.astype(bf16)
+        high = sine.astype(bf16)
+        twist[k, :trials, :CH] = low
+        twist[k, :trials, CH:] = -high
+        twist[k, trials:, :CH] = high
+        twist[k, trials:, CH:] = low
+        cosine, sine = cosine * cos_one - sine * sin_one, sine * cos_one + cosine * sin_one
+
+    sums[...] = jnp.zeros_like(sums)
+    start = 1.0 + (me * local).astype(f32) * (1.0 / CH)
+    own.wait()
+
+    def steer(source):
+        at = pl.multiple_of(source * LANES, LANES)
+        antenna = lax.broadcasted_iota(jnp.int32, (INPUTS, LANES), 0)
+        pick = jnp.where(antenna == order[:, pl.ds(at, LANES)], 1.0, 0.0).astype(bf16)
+        placed = None
+        for index in range(3):
+            term = jnp.dot(parts[index], pick, preferred_element_type=f32)
+            placed = term if placed is None else placed + term
+        placed = jnp.concatenate([placed] * (LANES // 16), axis=0).T
+        columns = BEAMS // 2
+        for block in range(LANES // 16):
+            p = placed[block * 16 : (block + 1) * 16]
+            for side in range(2):
+                lanes = slice(side * columns, (side + 1) * columns)
+                turns = p[:, 0:1] * directions[0:1, lanes]
+                turns = turns + p[:, 1:2] * directions[1:2, lanes]
+                turns = turns + p[:, 2:3] * directions[2:3, lanes]
+                cosine, sine = turn(turns * start)
+                cos_step, sin_step = turn(turns * (1.0 / CH))
+                real, imag = cosine, -sine
+                for c in range(local):
+                    wheel[c, block * 16 : (block + 1) * 16, lanes] = real.astype(bf16)
+                    wheel[c, LANES + block * 16 : LANES + (block + 1) * 16, lanes] = imag.astype(bf16)
+                    if c + 1 < local:
+                        real, imag = (
+                            real * cos_step + imag * sin_step,
+                            imag * cos_step - real * sin_step,
+                        )
+
+    def add_source(step, carry):
+        source = lax.rem(me - step + n, n)
+        steer(source)
+
+        @pl.when(step > 0)
+        def _():
+            turned(step).wait_recv()
+
+        at = pl.multiple_of(source * LANES, LANES)
+
+        def add_channel(c, inner):
+            gain = gains[c, :, pl.ds(at, LANES)] * (1.0 / math.sqrt(INPUTS))
+            gain_real, gain_imag = gain[0:1], gain[1:2]
+            real = held[step, 2 * c].astype(f32)
+            imag = held[step, 2 * c + 1].astype(f32)
+            y_real = (gain_real * real - gain_imag * imag).astype(bf16)
+            y_imag = (gain_real * imag + gain_imag * real).astype(bf16)
+            left = jnp.concatenate(
+                [
+                    jnp.concatenate([y_real, -y_imag], axis=1),
+                    jnp.concatenate([y_imag, y_real], axis=1),
+                ],
+                axis=0,
+            )
+            sums[c] += jnp.dot(left, wheel[c], preferred_element_type=f32)
+            return inner
+
+        lax.fori_loop(0, local, add_channel, 0, unroll=4)
+        return carry
+
+    lax.fori_loop(0, n, add_source, 0)
+
+    def detect(c, carry):
+        total = sums[c]
+        power[c] = total[:TIME] * total[:TIME] + total[TIME:] * total[TIME:]
+        return carry
+
+    lax.fori_loop(0, local, detect, 0)
+    flat = power[...].reshape(local * TIME, BEAMS)
+    high = flat.astype(bf16)
+    low = (flat - high.astype(f32)).astype(bf16)
+    chosen = jnp.dot(high, onehot[...], preferred_element_type=f32) + jnp.dot(
+        low, onehot[...], preferred_element_type=f32
+    )
+    chosen = chosen.reshape(local, TIME, TIME * SEARCH) * spread[...][None]
+    mine[...] = jnp.sum(chosen, axis=1).astype(bf16)
+    here = pl.ds(pl.multiple_of(me * local, local), local)
+    gathered[here, :] = mine[...]
+
+    def shared(step):
+        return pltpu.make_async_remote_copy(
+            src_ref=mine,
+            dst_ref=gathered.at[here],
+            send_sem=share_send.at[step],
+            recv_sem=share_recv.at[step],
+            device_id={"crate": peer(step)},
+            device_id_type=MESH,
+        )
+
+    def share(step, carry):
+        shared(step).start()
+        return carry
+
+    def drain(step, carry):
+        turned(step).wait_send()
+        return carry
+
+    def arrive(step, carry):
+        shared(step).wait()
+        return carry
+
+    lax.fori_loop(1, n, share, 0)
+    lax.fori_loop(1, n, drain, 0)
+    lax.fori_loop(1, n, arrive, 0)
+
+    everything = gathered[...]
+    right = jnp.concatenate([everything[:, : half * SEARCH], everything[:, half * SEARCH :]], axis=0)
+    bins = lax.broadcasted_iota(jnp.int32, (2 * trials, half * SEARCH), 1) // SEARCH
+    out = jnp.zeros((2 * trials, half * SEARCH), f32)
+    for k in range(half):
+        out = jnp.where(bins == k, jnp.dot(twist[k], right, preferred_element_type=f32), out)
+    plane[...] = out
+
+
+def crate_device(n, voltages, gains, positions, directions, input_order, delays, search_beams):
+    window, dft, spread = constant_tables()
+    local = CH // n
+    rows = 2 * local
+    trials = TRIALS // n
+    half = TIME // 2
+    f32, bf16 = jnp.float32, jnp.bfloat16
+    vmem = pl.BlockSpec(memory_space=pltpu.VMEM)
+    power, plane = pl.pallas_call(
+        functools.partial(crate_kernel, n),
+        out_shape=(
+            jax.ShapeDtypeStruct((local, TIME, BEAMS), f32),
+            jax.ShapeDtypeStruct((2 * trials, half * SEARCH), f32),
+        ),
+        in_specs=[vmem] * 10,
+        out_specs=(vmem, vmem),
+        scratch_shapes=[
+            pltpu.VMEM((TIME, LANES, FFTLEN), bf16),
+            pltpu.VMEM((TIME * 2 * CH, LANES), f32),
+            pltpu.VMEM((n, rows, TIME, LANES), bf16),
+            pltpu.VMEM((n, rows, TIME, LANES), bf16),
+            pltpu.VMEM((3, 16, INPUTS), bf16),
+            pltpu.VMEM((local, 2 * LANES, BEAMS), bf16),
+            pltpu.VMEM((local, 2 * TIME, BEAMS), f32),
+            pltpu.VMEM((half, 2 * trials, 2 * CH), bf16),
+            pltpu.VMEM((BEAMS, TIME * SEARCH), bf16),
+            pltpu.VMEM((local, TIME * SEARCH), bf16),
+            pltpu.VMEM((CH, TIME * SEARCH), bf16),
+            pltpu.SemaphoreType.DMA((n,)),
+            pltpu.SemaphoreType.DMA((n,)),
+            pltpu.SemaphoreType.DMA,
+            pltpu.SemaphoreType.DMA((n,)),
+            pltpu.SemaphoreType.DMA((n,)),
+        ],
+        compiler_params=pltpu.CompilerParams(
+            collective_id=0, has_side_effects=True, vmem_limit_bytes=56 * 1024 * 1024
+        ),
+    )(
+        voltages,
+        jnp.asarray(window),
+        jnp.asarray(dft),
+        gains,
+        jnp.pad(positions, ((0, 13), (0, 0))),
+        directions,
+        input_order[None, :],
+        delays,
+        jnp.tile(search_beams, TIME)[None, :],
+        jnp.asarray(spread),
+    )
+    plane = plane.reshape(2, trials, half, SEARCH).transpose(1, 3, 0, 2)
+    return jnp.swapaxes(power, 1, 2), plane.reshape(trials, SEARCH, TIME)
+
+
 def solution(mesh):
     in_specs = (P(("groups", "crate"), None), P("crate", None, None), P(), P(), P(), P(), P())
     out_specs = (P(("groups", "crate"), None, None), P(("groups", "crate"), None, None))
-    return jax.shard_map(
-        on_device, mesh=mesh, in_specs=in_specs, out_specs=out_specs, check_vma=False
-    )
+    n = mesh.shape["crate"]
+    fits = INPUTS // n == LANES and (CH // n) % 16 == 0 and (TRIALS // n) % 16 == 0
+    body = functools.partial(crate_device, n) if fits else plain_device
+    return jax.shard_map(body, mesh=mesh, in_specs=in_specs, out_specs=out_specs, check_vma=False)

time: 857 us -> 143 us (0.17); the launches traced: 847 us -> 143 us
  other arithmetic: 544 us -> 0 us
  Pallas kernels: 0 us -> 135 us
  local copies, waits for them, and re-layouts: 96.2 us -> 7.07 us
  matrix products: 71.6 us -> 0 us
  waiting for transfers between devices: 69.7 us -> 0 us
  blocking collectives: 45.4 us -> 0 us
  loops' own time: 11.3 us -> 0 us
    convert_element_type x16 -> x0, other arithmetic: 275 us -> none  [steering(): ((gain_row[1] * cosine - gain_row[0] * sine_part) * weight_norm).astype(j...]
    neg x16 -> x0, other arithmetic: 266 us -> none  [steering(): upper_rows = jnp.concatenate([w_real, -w_imag], axis=1)]
    pallas_call x0 -> x1, Pallas kernels: none -> 135 us  [crate_device(): pl.pallas_call(functools.partial(crate_kernel, n), out_shape=(jax.ShapeDt...]
    dot_general x22 -> x0, matrix products: 71.6 us -> none  [the longest x16 40.2 us: one_channel(): jnp.dot(weights, channel_data.reshape(2 * INPUTS, channel_data.shape[-1])...]
    all_to_all x1 -> x0, waiting for transfers between devices: 69.7 us -> none  [on_device(): lax.all_to_all(spectra, 'crate', split_axis=0, concat_axis=2, tiled=True)]
    all_gather x1 -> x0, blocking collectives: 45.4 us -> none  [on_device(): lax.all_gather(power_spectra, 'crate', axis=0, tiled=True)]
    dynamic_slice x33 -> x0, local copies, waits for them, and re-layouts: 30.2 us -> none  [the longest x32 30.2 us: on_device(): lax.map(one_channel, (jnp.arange(local_count, dtype=jnp.int32), turned, g...]
    all_to_all x1 -> x0, local copies, waits for them, and re-layouts: 18.8 us -> none  [on_device(): lax.all_to_all(spectra, 'crate', split_axis=0, concat_axis=2, tiled=True)]
  transfers between devices with their start and end apart: 1 -> 0, of which waited for: 1 -> 0; matrix products, arithmetic and copies ran while one was open for 1% -> 0% of each run, Pallas kernels for 0% -> 0%
where the time goes in v1:
time: 143 us
  Pallas kernels  135 us (94%)
  local copies, waits for them, and re-layouts  7.07 us (5%)
    pallas_call x1, Pallas kernels, crate_device(): pl.pallas_call(functools.partial(crate_kernel, n), out_shape=(jax.ShapeDt...  135 us

profile of v1, /device:TPU:0, one launch (start us, length us, event | category | flops | bytes accessed | tf_op | source)
XLA Modules:
  0.0 143.1 jit_solution(16673238693731941034)
XLA Ops:
  0.6 0.7 tile.2
  1.3 0.7 broadcast_in_dim_tile.3.beams
  1.9 1.4 pad.4.positions
  3.4 135.4 %shard_map.113 = (f32[16,32,512]{2,1,0:T(8,128)}, f32[128,256]{1,0:T(8,128)}) custom-call(bf16[128,17920]{1,0:T(8,128)(2,1)} %volts.1, f32[4,512]{1,0:T(4,128)} %constant.9.clone.window, bf16[512,512]{1,0:T(8,128)(2,1)} %constant.10.clone.dft, f32[16,2,2048]{2,1,0:T(2,128)} %gains.1, f32[16,2048]{1,0:T(8,128)} %pad.4.positions, f32[3,512]{1,0:T(4,128)} %directions.1, ...), custom_call_target="tpu_custom_call" | custom-call | tf_op jit(solution)/shard_map/pallas_call | solution.py:399
  138.8 1.0 copy.14
  139.8 0.2 reshape.11
  140.0 0.9 copy.15
  140.8 2.3 %copy.17 = f32[16,512,32]{1,2,0:T(8,128)} copy(f32[16,512,32]{1,2,0:T(8,128)} %bitcast.6) | data formatting | bytes 2097152

commit v2 on v1

--- a/solution.py
+++ b/solution.py
@@ -151,12 +151,15 @@
     s = np.arange(FFTLEN)[None, :]
     angles = TWO_PI * (c * s % FFTLEN) / FFTLEN
     table = np.stack([np.cos(angles), -np.sin(angles)], axis=1) / math.sqrt(FFTLEN)
-    dft = table.reshape(2 * CH, FFTLEN).astype(jnp.bfloat16)
+    dft = table.reshape(2 * CH, FFTLEN).astype(np.float32)
     t = np.arange(TIME)[:, None]
     k = np.arange(1, TIME // 2 + 1)[None, :]
     turns = TWO_PI * (t * k % TIME) / TIME
     steps = np.concatenate([np.cos(turns), -np.sin(turns)], axis=1) / math.sqrt(TIME * CH)
-    spread = np.repeat(steps, SEARCH, axis=1).astype(np.float32)
+    spread = np.concatenate(
+        [np.tile(steps[:, : TIME // 2], (1, SEARCH)), np.tile(steps[:, TIME // 2 :], (1, SEARCH))],
+        axis=1,
+    ).astype(np.float32)
     return window, dft, spread
 
 
@@ -183,7 +186,7 @@
 def crate_kernel(
     n, volts, window, dft, gains, positions, directions, order, delays, beams, spread,
     power, plane,
-    folded, frames, sent, held, parts, wheel, sums, twist, onehot, mine, gathered,
+    table, frames, sent, held, parts, columns, wheel, sums, twist, onehot, mine, gathered,
     send_sem, recv_sem, own_sem, share_send, share_recv,
 ):
     me = lax.axis_index("crate")
@@ -204,28 +207,27 @@
 
     lax.fori_loop(1, n, greet, 0)
 
-    def fold(t, carry):
+    table[...] = dft[...].astype(bf16)
+
+    def fold(t):
         total = None
         for tap in range(TAPS):
             at = pl.multiple_of((t + tap) * FFTLEN, FFTLEN)
             term = window[tap : tap + 1, :] * volts[:, pl.ds(at, FFTLEN)].astype(f32)
             total = term if total is None else total + term
-        folded[t] = total.astype(bf16)
-        return carry
-
-    lax.fori_loop(0, TIME, fold, 0)
+        return total.astype(bf16)
 
     def channelize(pair, carry):
-        block = folded[pl.ds(2 * pair, 2)].reshape(2 * LANES, FFTLEN)
+        block = jnp.concatenate([fold(2 * pair), fold(2 * pair + 1)], axis=0)
         out = lax.dot_general(
-            dft[...], block, (((1,), (1,)), ((), ())), preferred_element_type=f32
+            table[...], block, (((1,), (1,)), ((), ())), preferred_element_type=f32
         )
         for which in range(2):
             at = pl.multiple_of((2 * pair + which) * 2 * CH, 2 * CH)
             frames[pl.ds(at, 2 * CH), :] = out[:, which * LANES : (which + 1) * LANES]
         return carry
 
-    lax.fori_loop(0, TIME // 2, channelize, 0)
+    lax.fori_loop(0, TIME // 2, channelize, 0, unroll=2)
 
     def pack(step):
         first = peer(step) * rows
@@ -254,10 +256,15 @@
     own = pltpu.make_async_copy(sent.at[0], held.at[0], own_sem)
     own.start()
 
+    parts[...] = jnp.zeros_like(parts)
     for index, part in enumerate(split_three(positions[...])):
-        parts[index] = part
-    beam_ids = lax.broadcasted_iota(jnp.int32, (BEAMS, TIME * SEARCH), 0)
-    onehot[...] = jnp.where(beam_ids == beams[...], 1.0, 0.0).astype(bf16)
+        parts[16 * index : 16 * index + 3] = part
+    beam_ids = lax.broadcasted_iota(jnp.int32, (BEAMS, SEARCH), 0)
+    listed = jnp.where(beam_ids == beams[...], 1.0, 0.0).astype(bf16)
+    search_ids = lax.broadcasted_iota(jnp.int32, (SEARCH, TIME * SEARCH), 0)
+    lane_ids = lax.broadcasted_iota(jnp.int32, (SEARCH, TIME * SEARCH), 1)
+    widen = jnp.where(lane_ids // half % SEARCH == search_ids, 1.0, 0.0).astype(bf16)
+    onehot[...] = jnp.dot(listed, widen, preferred_element_type=f32).astype(bf16)
 
     at = pl.multiple_of(me * trials, trials)
     cos_one, sin_one = turn(delays[pl.ds(at, trials), :].astype(f32) * (1.0 / TIME))
@@ -275,66 +282,90 @@
     start = 1.0 + (me * local).astype(f32) * (1.0 / CH)
     own.wait()
 
-    def steer(source):
+    def place(source):
         at = pl.multiple_of(source * LANES, LANES)
         antenna = lax.broadcasted_iota(jnp.int32, (INPUTS, LANES), 0)
         pick = jnp.where(antenna == order[:, pl.ds(at, LANES)], 1.0, 0.0).astype(bf16)
-        placed = None
-        for index in range(3):
-            term = jnp.dot(parts[index], pick, preferred_element_type=f32)
-            placed = term if placed is None else placed + term
-        placed = jnp.concatenate([placed] * (LANES // 16), axis=0).T
-        columns = BEAMS // 2
-        for block in range(LANES // 16):
-            p = placed[block * 16 : (block + 1) * 16]
-            for side in range(2):
-                lanes = slice(side * columns, (side + 1) * columns)
-                turns = p[:, 0:1] * directions[0:1, lanes]
-                turns = turns + p[:, 1:2] * directions[1:2, lanes]
-                turns = turns + p[:, 2:3] * directions[2:3, lanes]
-                cosine, sine = turn(turns * start)
-                cos_step, sin_step = turn(turns * (1.0 / CH))
-                real, imag = cosine, -sine
-                for c in range(local):
-                    wheel[c, block * 16 : (block + 1) * 16, lanes] = real.astype(bf16)
-                    wheel[c, LANES + block * 16 : LANES + (block + 1) * 16, lanes] = imag.astype(bf16)
-                    if c + 1 < local:
-                        real, imag = (
-                            real * cos_step + imag * sin_step,
-                            imag * cos_step - real * sin_step,
-                        )
-
-    def add_source(step, carry):
-        source = lax.rem(me - step + n, n)
-        steer(source)
-
+        out = jnp.dot(parts[...], pick, preferred_element_type=f32)
+        placed = out[0:16] + out[16:32] + out[32:48]
+        columns[...] = jnp.concatenate([placed] * (LANES // 16), axis=0).T
+
+    def steer(block, slot):
+        first = pl.multiple_of(block * 16, 16)
+        p = columns[pl.ds(first, 16), :]
+        width = BEAMS // 2
+        for side in range(2):
+            lanes = slice(side * width, (side + 1) * width)
+            turns = p[:, 0:1] * directions[0:1, lanes]
+            turns = turns + p[:, 1:2] * directions[1:2, lanes]
+            turns = turns + p[:, 2:3] * directions[2:3, lanes]
+            cosine, sine = turn(turns * start)
+            cos_step, sin_step = turn(turns * (1.0 / CH))
+            real, imag = cosine, -sine
+            ahead = (real * cos_step + imag * sin_step, imag * cos_step - real * sin_step)
+            twice = 2.0 * cos_step
+            for c in range(local):
+                wheel[slot, c, pl.ds(first, 16), lanes] = real.astype(bf16)
+                wheel[slot, c, pl.ds(LANES + first, 16), lanes] = imag.astype(bf16)
+                if c + 1 < local:
+                    after = (twice * ahead[0] - real, twice * ahead[1] - imag)
+                    (real, imag), ahead = ahead, after
+
+    def add_channel(c, step, slot, at):
+        gain = gains[c, :, pl.ds(at, LANES)] * (1.0 / math.sqrt(INPUTS))
+        gain_real, gain_imag = gain[0:1], gain[1:2]
+        real = held[step, 2 * c].astype(f32)
+        imag = held[step, 2 * c + 1].astype(f32)
+        y_real = (gain_real * real - gain_imag * imag).astype(bf16)
+        y_imag = (gain_real * imag + gain_imag * real).astype(bf16)
+        left = jnp.concatenate(
+            [
+                jnp.concatenate([y_real, -y_imag], axis=1),
+                jnp.concatenate([y_imag, y_real], axis=1),
+            ],
+            axis=0,
+        )
+        sums[c] += jnp.dot(left, wheel[slot, c], preferred_element_type=f32)
+
+    blocks = LANES // 16
+    per_block = local // blocks
+
+    def owner(step):
+        return lax.rem(me - step + n, n)
+
+    def add_source(step, steering_on):
+        slot = lax.rem(step, 2)
+        at = pl.multiple_of(owner(step) * LANES, LANES)
+        if steering_on:
+            place(owner(step + 1))
+
+        def body(block, carry):
+            if steering_on:
+                steer(block, 1 - slot)
+            for c in range(per_block):
+                add_channel(block * per_block + c, step, slot, at)
+            return carry
+
+        lax.fori_loop(0, blocks, body, 0, unroll=1 if steering_on else 4)
+
+    def first_steer(block, carry):
+        steer(block, 0)
+        return carry
+
+    place(me)
+    lax.fori_loop(0, blocks, first_steer, 0)
+
+    def middle(step, carry):
         @pl.when(step > 0)
         def _():
             turned(step).wait_recv()
 
-        at = pl.multiple_of(source * LANES, LANES)
-
-        def add_channel(c, inner):
-            gain = gains[c, :, pl.ds(at, LANES)] * (1.0 / math.sqrt(INPUTS))
-            gain_real, gain_imag = gain[0:1], gain[1:2]
-            real = held[step, 2 * c].astype(f32)
-            imag = held[step, 2 * c + 1].astype(f32)
-            y_real = (gain_real * real - gain_imag * imag).astype(bf16)
-            y_imag = (gain_real * imag + gain_imag * real).astype(bf16)
-            left = jnp.concatenate(
-                [
-                    jnp.concatenate([y_real, -y_imag], axis=1),
-                    jnp.concatenate([y_imag, y_real], axis=1),
-                ],
-                axis=0,
-            )
-            sums[c] += jnp.dot(left, wheel[c], preferred_element_type=f32)
-            return inner
-
-        lax.fori_loop(0, local, add_channel, 0, unroll=4)
-        return carry
-
-    lax.fori_loop(0, n, add_source, 0)
+        add_source(step, True)
+        return carry
+
+    lax.fori_loop(0, n - 1, middle, 0)
+    turned(n - 1).wait_recv()
+    add_source(n - 1, False)
 
     def detect(c, carry):
         total = sums[c]
@@ -381,11 +412,13 @@
 
     everything = gathered[...]
     right = jnp.concatenate([everything[:, : half * SEARCH], everything[:, half * SEARCH :]], axis=0)
-    bins = lax.broadcasted_iota(jnp.int32, (2 * trials, half * SEARCH), 1) // SEARCH
+    bins = lax.broadcasted_iota(jnp.int32, (2 * trials, half * SEARCH), 1) % half
     out = jnp.zeros((2 * trials, half * SEARCH), f32)
     for k in range(half):
         out = jnp.where(bins == k, jnp.dot(twist[k], right, preferred_element_type=f32), out)
-    plane[...] = out
+    out = out.T.reshape(SEARCH, half, 2 * trials)
+    plane[:, :half, :] = out[:, :, :trials]
+    plane[:, half:, :] = out[:, :, trials:]
 
 
 def crate_device(n, voltages, gains, positions, directions, input_order, delays, search_beams):
@@ -400,17 +433,18 @@
         functools.partial(crate_kernel, n),
         out_shape=(
             jax.ShapeDtypeStruct((local, TIME, BEAMS), f32),
-            jax.ShapeDtypeStruct((2 * trials, half * SEARCH), f32),
+            jax.ShapeDtypeStruct((SEARCH, TIME, trials), f32),
         ),
         in_specs=[vmem] * 10,
         out_specs=(vmem, vmem),
         scratch_shapes=[
-            pltpu.VMEM((TIME, LANES, FFTLEN), bf16),
+            pltpu.VMEM((2 * CH, FFTLEN), bf16),
             pltpu.VMEM((TIME * 2 * CH, LANES), f32),
             pltpu.VMEM((n, rows, TIME, LANES), bf16),
             pltpu.VMEM((n, rows, TIME, LANES), bf16),
-            pltpu.VMEM((3, 16, INPUTS), bf16),
-            pltpu.VMEM((local, 2 * LANES, BEAMS), bf16),
+            pltpu.VMEM((48, INPUTS), bf16),
+            pltpu.VMEM((LANES, LANES), f32),
+            pltpu.VMEM((2, local, 2 * LANES, BEAMS), bf16),
             pltpu.VMEM((local, 2 * TIME, BEAMS), f32),
             pltpu.VMEM((half, 2 * trials, 2 * CH), bf16),
             pltpu.VMEM((BEAMS, TIME * SEARCH), bf16),
@@ -430,15 +464,14 @@
         jnp.asarray(window),
         jnp.asarray(dft),
         gains,
-        jnp.pad(positions, ((0, 13), (0, 0))),
+        positions,
         directions,
         input_order[None, :],
         delays,
-        jnp.tile(search_beams, TIME)[None, :],
+        search_beams[None, :],
         jnp.asarray(spread),
     )
-    plane = plane.reshape(2, trials, half, SEARCH).transpose(1, 3, 0, 2)
-    return jnp.swapaxes(power, 1, 2), plane.reshape(trials, SEARCH, TIME)
+    return jnp.swapaxes(power, 1, 2), plane.transpose(2, 0, 1)
 
 
 def solution(mesh):

time: 143 us -> 143 us (level)
  local copies, waits for them, and re-layouts: 7.07 us -> 3.96 us
  Pallas kernels: 135 us -> 138 us
    pallas_call x1, Pallas kernels: 135 us -> 138 us  [crate_device(): pl.pallas_call(functools.partial(crate_kernel, n), out_shape=(jax.ShapeDt...]
    unnamed x1 -> x2, local copies, waits for them, and re-layouts: 2.29 us -> 3.96 us
where the time goes in v2:
time: 143 us
  Pallas kernels  138 us (97%)
  local copies, waits for them, and re-layouts  3.96 us (3%)
    pallas_call x1, Pallas kernels, crate_device(): pl.pallas_call(functools.partial(crate_kernel, n), out_shape=(jax.ShapeDt...  138 us
    unnamed x2, local copies, waits for them, and re-layouts  3.96 us

profile of v2, /device:TPU:0, one launch (start us, length us, event | category | flops | bytes accessed | tf_op | source)
XLA Modules:
  0.0 143.1 jit_solution(17386085394143016927)
XLA Ops:
  0.6 138.5 %shard_map.113 = (f32[16,32,512]{2,1,0:T(8,128)}, f32[16,32,64]{2,1,0:T(8,128)}) custom-call(bf16[128,17920]{1,0:T(8,128)(2,1)} %volts.1, f32[4,512]{1,0:T(4,128)} %constant.6.clone.window, f32[512,512]{1,0:T(8,128)} %constant.7.clone.dft, f32[16,2,2048]{2,1,0:T(2,128)} %gains.1, f32[3,2048]{1,0:T(4,128)} %positions.1, f32[3,512]{1,0:T(4,128)} %directions.1, ...), custom_call_target="tpu_custom_call" | custom-call | tf_op jit(solution)/shard_map/pallas_call | solution.py:432
  139.1 2.3 %copy.14 = f32[16,512,32]{1,2,0:T(8,128)} copy(f32[16,512,32]{1,2,0:T(8,128)} %bitcast.4) | data formatting | bytes 2097152
  141.4 1.7 %copy.15 = f32[64,16,32]{0,2,1:T(8,128)} copy(f32[64,16,32]{0,2,1:T(8,128)} %bitcast.5) | data formatting | bytes 262144

commit v3 on v2

--- a/solution.py
+++ b/solution.py
@@ -187,7 +187,8 @@
     n, volts, window, dft, gains, positions, directions, order, delays, beams, spread,
     power, plane,
     table, frames, sent, held, parts, columns, wheel, sums, twist, onehot, mine, gathered,
-    send_sem, recv_sem, own_sem, share_send, share_recv,
+    lent, leaving, landing,
+    send_sem, recv_sem, own_sem, share_send, share_recv, lend_sem, part_send, part_recv,
 ):
     me = lax.axis_index("crate")
     rows = 2 * CH // n
@@ -196,8 +197,22 @@
     half = TIME // 2
     f32, bf16 = jnp.float32, jnp.bfloat16
 
+    m = n // 2
+    side = me // m
+    place_in = lax.rem(me, m)
+    twin = (1 - side) * m + place_in
+
     def peer(step):
         return lax.rem(me + step, n)
+
+    def near(u):
+        return side * m + lax.rem(place_in + u, m)
+
+    def owner(u):
+        return side * m + lax.rem(place_in - u + 2 * m, m)
+
+    def channel_side(u):
+        return side + (1 - u // m) * (1 - 2 * side)
 
     barrier = pltpu.get_barrier_semaphore()
 
@@ -229,32 +244,56 @@
 
     lax.fori_loop(0, TIME // 2, channelize, 0, unroll=2)
 
-    def pack(step):
-        first = peer(step) * rows
+    def pack(u):
+        first = (channel_side(u) * m + lax.rem(place_in + u, m)) * rows
         for row in range(rows):
-            sent[step, row] = frames[pl.ds(first + row, TIME, stride=2 * CH), :].astype(bf16)
-
-    def turned(step):
+            sent[u, row] = frames[pl.ds(first + row, TIME, stride=2 * CH), :].astype(bf16)
+
+    def turned(u):
         return pltpu.make_async_remote_copy(
-            src_ref=sent.at[step],
-            dst_ref=held.at[step],
-            send_sem=send_sem.at[step],
-            recv_sem=recv_sem.at[step],
-            device_id={"crate": peer(step)},
+            src_ref=sent.at[u],
+            dst_ref=held.at[u],
+            send_sem=send_sem.at[u],
+            recv_sem=recv_sem.at[u],
+            device_id={"crate": near(u)},
             device_id_type=MESH,
         )
 
+    def partial(c):
+        return pltpu.make_async_remote_copy(
+            src_ref=leaving.at[c],
+            dst_ref=landing.at[c],
+            send_sem=part_send.at[c],
+            recv_sem=part_recv.at[c],
+            device_id={"crate": twin},
+            device_id_type=MESH,
+        )
+
+    far = pl.ds(pl.multiple_of((1 - side) * (m * LANES), LANES), m * LANES)
+    lend = pltpu.make_async_remote_copy(
+        src_ref=gains.at[:, :, far],
+        dst_ref=lent,
+        send_sem=lend_sem.at[0],
+        recv_sem=lend_sem.at[1],
+        device_id={"crate": twin},
+        device_id_type=MESH,
+    )
     pl.semaphore_wait(barrier, n - 1)
-
-    def send(step, carry):
-        pack(step)
-        turned(step).start()
-        return carry
-
-    lax.fori_loop(1, n, send, 0)
+    lend.start()
+
+    def send(u, carry):
+        pack(u)
+        turned(u).start()
+        return carry
+
+    lax.fori_loop(1, m, send, 0)
     pack(0)
-    own = pltpu.make_async_copy(sent.at[0], held.at[0], own_sem)
-    own.start()
+    own_first = pltpu.make_async_copy(sent.at[0], held.at[0], own_sem.at[0])
+    own_first.start()
+    lax.fori_loop(m + 1, n, send, 0)
+    pack(m)
+    own_later = pltpu.make_async_copy(sent.at[m], held.at[m], own_sem.at[1])
+    own_later.start()
 
     parts[...] = jnp.zeros_like(parts)
     for index, part in enumerate(split_three(positions[...])):
@@ -279,8 +318,8 @@
         cosine, sine = cosine * cos_one - sine * sin_one, sine * cos_one + cosine * sin_one
 
     sums[...] = jnp.zeros_like(sums)
-    start = 1.0 + (me * local).astype(f32) * (1.0 / CH)
-    own.wait()
+    own_first.wait()
+    own_later.wait()
 
     def place(source):
         at = pl.multiple_of(source * LANES, LANES)
@@ -290,7 +329,9 @@
         placed = out[0:16] + out[16:32] + out[32:48]
         columns[...] = jnp.concatenate([placed] * (LANES // 16), axis=0).T
 
-    def steer(block, slot):
+    def steer(block, slot, u):
+        first_channel = (channel_side(u) * m + place_in) * local
+        start = 1.0 + first_channel.astype(f32) * (1.0 / CH)
         first = pl.multiple_of(block * 16, 16)
         p = columns[pl.ds(first, 16), :]
         width = BEAMS // 2
@@ -311,8 +352,8 @@
                     after = (twice * ahead[0] - real, twice * ahead[1] - imag)
                     (real, imag), ahead = ahead, after
 
-    def add_channel(c, step, slot, at):
-        gain = gains[c, :, pl.ds(at, LANES)] * (1.0 / math.sqrt(INPUTS))
+    def add_channel(c, step, slot, gain_ref, at):
+        gain = gain_ref[c, :, pl.ds(at, LANES)] * (1.0 / math.sqrt(INPUTS))
         gain_real, gain_imag = gain[0:1], gain[1:2]
         real = held[step, 2 * c].astype(f32)
         imag = held[step, 2 * c + 1].astype(f32)
@@ -330,45 +371,60 @@
     blocks = LANES // 16
     per_block = local // blocks
 
-    def owner(step):
-        return lax.rem(me - step + n, n)
-
-    def add_source(step, steering_on):
-        slot = lax.rem(step, 2)
-        at = pl.multiple_of(owner(step) * LANES, LANES)
+    def add_source(u, later, steering_on):
+        slot = lax.rem(u, 2)
+        gain_ref = gains if later else lent
+        source = owner(u) if later else owner(u) - side * m
+        at = pl.multiple_of(source * LANES, LANES)
         if steering_on:
-            place(owner(step + 1))
+            place(owner(u + 1))
 
         def body(block, carry):
             if steering_on:
-                steer(block, 1 - slot)
+                steer(block, 1 - slot, u + 1)
             for c in range(per_block):
-                add_channel(block * per_block + c, step, slot, at)
+                add_channel(block * per_block + c, u, slot, gain_ref, at)
             return carry
 
         lax.fori_loop(0, blocks, body, 0, unroll=1 if steering_on else 4)
 
     def first_steer(block, carry):
-        steer(block, 0)
+        steer(block, 0, 0)
         return carry
 
     place(me)
     lax.fori_loop(0, blocks, first_steer, 0)
-
-    def middle(step, carry):
-        @pl.when(step > 0)
-        def _():
-            turned(step).wait_recv()
-
-        add_source(step, True)
-        return carry
-
-    lax.fori_loop(0, n - 1, middle, 0)
+    lend.wait()
+    add_source(0, False, True)
+
+    def for_twin(u, carry):
+        turned(u).wait_recv()
+        add_source(u, False, True)
+        return carry
+
+    lax.fori_loop(1, m, for_twin, 0)
+
+    def hand_over(c, carry):
+        leaving[c] = sums[c].astype(bf16)
+        partial(c).start()
+        sums[c] = jnp.zeros((2 * TIME, BEAMS), f32)
+        return carry
+
+    lax.fori_loop(0, local, hand_over, 0)
+    add_source(m, True, True)
+
+    def for_self(u, carry):
+        turned(u).wait_recv()
+        add_source(u, True, True)
+        return carry
+
+    lax.fori_loop(m + 1, n - 1, for_self, 0)
     turned(n - 1).wait_recv()
-    add_source(n - 1, False)
+    add_source(n - 1, True, False)
 
     def detect(c, carry):
-        total = sums[c]
+        partial(c).wait()
+        total = sums[c] + landing[c].astype(f32)
         power[c] = total[:TIME] * total[:TIME] + total[TIME:] * total[TIME:]
         return carry
 
@@ -398,8 +454,8 @@
         shared(step).start()
         return carry
 
-    def drain(step, carry):
-        turned(step).wait_send()
+    def drain(u, carry):
+        turned(u).wait_send()
         return carry
 
     def arrive(step, carry):
@@ -407,7 +463,8 @@
         return carry
 
     lax.fori_loop(1, n, share, 0)
-    lax.fori_loop(1, n, drain, 0)
+    lax.fori_loop(1, m, drain, 0)
+    lax.fori_loop(m + 1, n, drain, 0)
     lax.fori_loop(1, n, arrive, 0)
 
     everything = gathered[...]
@@ -450,11 +507,17 @@
             pltpu.VMEM((BEAMS, TIME * SEARCH), bf16),
             pltpu.VMEM((local, TIME * SEARCH), bf16),
             pltpu.VMEM((CH, TIME * SEARCH), bf16),
+            pltpu.VMEM((local, 2, INPUTS // 2), f32),
+            pltpu.VMEM((local, 2 * TIME, BEAMS), bf16),
+            pltpu.VMEM((local, 2 * TIME, BEAMS), bf16),
             pltpu.SemaphoreType.DMA((n,)),
             pltpu.SemaphoreType.DMA((n,)),
-            pltpu.SemaphoreType.DMA,
+            pltpu.SemaphoreType.DMA((2,)),
             pltpu.SemaphoreType.DMA((n,)),
             pltpu.SemaphoreType.DMA((n,)),
+            pltpu.SemaphoreType.DMA((2,)),
+            pltpu.SemaphoreType.DMA((local,)),
+            pltpu.SemaphoreType.DMA((local,)),
         ],
         compiler_params=pltpu.CompilerParams(
             collective_id=0, has_side_effects=True, vmem_limit_bytes=56 * 1024 * 1024
@@ -478,6 +541,6 @@
     in_specs = (P(("groups", "crate"), None), P("crate", None, None), P(), P(), P(), P(), P())
     out_specs = (P(("groups", "crate"), None, None), P(("groups", "crate"), None, None))
     n = mesh.shape["crate"]
-    fits = INPUTS // n == LANES and (CH // n) % 16 == 0 and (TRIALS // n) % 16 == 0
+    fits = n % 2 == 0 and INPUTS // n == LANES and (CH // n) % 16 == 0 and (TRIALS // n) % 16 == 0
     body = functools.partial(crate_device, n) if fits else plain_device
     return jax.shard_map(body, mesh=mesh, in_specs=in_specs, out_specs=out_specs, check_vma=False)

time: 143 us -> 113 us (0.79)
  Pallas kernels: 138 us -> 107 us
    pallas_call x1, Pallas kernels: 138 us -> 107 us  [crate_device(): pl.pallas_call(functools.partial(crate_kernel, n), out_shape=(jax.ShapeDt...]
where the time goes in v3:
time: 113 us; the launch traced here: 112 us
  Pallas kernels  107 us (95%)
  local copies, waits for them, and re-layouts  3.96 us (4%)
    pallas_call x1, Pallas kernels, crate_device(): pl.pallas_call(functools.partial(crate_kernel, n), out_shape=(jax.ShapeDt...  107 us
    unnamed x2, local copies, waits for them, and re-layouts  3.96 us

profile of v3, /device:TPU:0, one launch (start us, length us, event | category | flops | bytes accessed | tf_op | source)
XLA Modules:
  0.0 111.8 jit_solution(18149655669149260578)
XLA Ops:
  0.6 107.2 %shard_map.113 = (f32[16,32,512]{2,1,0:T(8,128)}, f32[16,32,64]{2,1,0:T(8,128)}) custom-call(bf16[128,17920]{1,0:T(8,128)(2,1)} %volts.1, f32[4,512]{1,0:T(4,128)} %constant.6.clone.window, f32[512,512]{1,0:T(8,128)} %constant.7.clone.dft, f32[16,2,2048]{2,1,0:T(2,128)} %gains.1, f32[3,2048]{1,0:T(4,128)} %positions.1, f32[3,512]{1,0:T(4,128)} %directions.1, ...), custom_call_target="tpu_custom_call" | custom-call | tf_op jit(solution)/shard_map/pallas_call | solution.py:489
  107.9 2.3 %copy.14 = f32[16,512,32]{1,2,0:T(8,128)} copy(f32[16,512,32]{1,2,0:T(8,128)} %bitcast.4) | data formatting | bytes 2097152
  110.1 1.7 %copy.15 = f32[64,16,32]{0,2,1:T(8,128)} copy(f32[64,16,32]{0,2,1:T(8,128)} %bitcast.5) | data formatting | bytes 262144

commit v4 on v3

--- a/solution.py
+++ b/solution.py
@@ -163,17 +163,28 @@
     return window, dft, spread
 
 
+def series(function, degree):
+    nodes = 0.125 + 0.125 * np.cos((2 * np.arange(400) + 1) * np.pi / 800)
+    fit = np.polynomial.chebyshev.Chebyshev.fit(nodes, function(nodes), degree, domain=[0, 0.25])
+    return [float(value) for value in fit.convert(kind=np.polynomial.Polynomial).coef[::-1]]
+
+
+SINE = series(lambda z: np.pi * np.sinc(np.sqrt(z)), 4)
+COSINE = series(lambda z: np.cos(np.pi * np.sqrt(z)), 4)
+ROUNDER = 1.5 * 2.0**23
+
+
 def turn(x):
-    y = (x - jnp.round(x)) * math.pi
+    y = x - ((x + ROUNDER) - ROUNDER)
     z = y * y
-    sine = 1.0 / math.factorial(11) * -1.0
-    for power in (9, 7, 5, 3, 1):
-        sine = sine * z + (-1.0) ** (power // 2) / math.factorial(power)
+    sine, cosine = SINE[0], COSINE[0]
+    for value in SINE[1:]:
+        sine = sine * z + value
+    for value in COSINE[1:]:
+        cosine = cosine * z + value
     sine = sine * y
-    cosine = 1.0 / math.factorial(12)
-    for power in (10, 8, 6, 4, 2, 0):
-        cosine = cosine * z + (-1.0) ** (power // 2) / math.factorial(power)
-    return 1.0 - 2.0 * sine * sine, 2.0 * sine * cosine
+    double = sine + sine
+    return 1.0 - double * sine, double * cosine
 
 
 def split_three(x):
@@ -186,7 +197,7 @@
 def crate_kernel(
     n, volts, window, dft, gains, positions, directions, order, delays, beams, spread,
     power, plane,
-    table, frames, sent, held, parts, columns, wheel, sums, twist, onehot, mine, gathered,
+    table, folded, frames, sent, held, parts, columns, wheel, sums, twist, onehot, mine, gathered,
     lent, leaving, landing,
     send_sem, recv_sem, own_sem, share_send, share_recv, lend_sem, part_send, part_recv,
 ):
@@ -223,6 +234,7 @@
     lax.fori_loop(1, n, greet, 0)
 
     table[...] = dft[...].astype(bf16)
+    side_rows = m * rows
 
     def fold(t):
         total = None
@@ -232,17 +244,25 @@
             total = term if total is None else total + term
         return total.astype(bf16)
 
-    def channelize(pair, carry):
-        block = jnp.concatenate([fold(2 * pair), fold(2 * pair + 1)], axis=0)
-        out = lax.dot_general(
-            table[...], block, (((1,), (1,)), ((), ())), preferred_element_type=f32
-        )
-        for which in range(2):
-            at = pl.multiple_of((2 * pair + which) * 2 * CH, 2 * CH)
-            frames[pl.ds(at, 2 * CH), :] = out[:, which * LANES : (which + 1) * LANES]
-        return carry
-
-    lax.fori_loop(0, TIME // 2, channelize, 0, unroll=2)
+    def channelize(which_side, first_time):
+        begin = pl.multiple_of(which_side * side_rows, side_rows)
+
+        def body(pair, carry):
+            if first_time:
+                folded[pair, :LANES] = fold(2 * pair)
+                folded[pair, LANES:] = fold(2 * pair + 1)
+            out = lax.dot_general(
+                table[pl.ds(begin, side_rows), :],
+                folded[pair],
+                (((1,), (1,)), ((), ())),
+                preferred_element_type=f32,
+            )
+            for which in range(2):
+                at = pl.multiple_of((2 * pair + which) * 2 * CH + begin, side_rows)
+                frames[pl.ds(at, side_rows), :] = out[:, which * LANES : (which + 1) * LANES]
+            return carry
+
+        lax.fori_loop(0, TIME // 2, body, 0, unroll=2)
 
     def pack(u):
         first = (channel_side(u) * m + lax.rem(place_in + u, m)) * rows
@@ -278,6 +298,7 @@
         device_id={"crate": twin},
         device_id_type=MESH,
     )
+    channelize(1 - side, True)
     pl.semaphore_wait(barrier, n - 1)
     lend.start()
 
@@ -290,6 +311,7 @@
     pack(0)
     own_first = pltpu.make_async_copy(sent.at[0], held.at[0], own_sem.at[0])
     own_first.start()
+    channelize(side, False)
     lax.fori_loop(m + 1, n, send, 0)
     pack(m)
     own_later = pltpu.make_async_copy(sent.at[m], held.at[m], own_sem.at[1])
@@ -321,19 +343,19 @@
     own_first.wait()
     own_later.wait()
 
-    def place(source):
-        at = pl.multiple_of(source * LANES, LANES)
+    def place(u):
+        at = pl.multiple_of(owner(u) * LANES, LANES)
         antenna = lax.broadcasted_iota(jnp.int32, (INPUTS, LANES), 0)
         pick = jnp.where(antenna == order[:, pl.ds(at, LANES)], 1.0, 0.0).astype(bf16)
         out = jnp.dot(parts[...], pick, preferred_element_type=f32)
         placed = out[0:16] + out[16:32] + out[32:48]
-        columns[...] = jnp.concatenate([placed] * (LANES // 16), axis=0).T
+        columns[lax.rem(u, m)] = jnp.concatenate([placed] * (LANES // 16), axis=0).T
 
     def steer(block, slot, u):
         first_channel = (channel_side(u) * m + place_in) * local
         start = 1.0 + first_channel.astype(f32) * (1.0 / CH)
         first = pl.multiple_of(block * 16, 16)
-        p = columns[pl.ds(first, 16), :]
+        p = columns[lax.rem(u, m), pl.ds(first, 16), :]
         width = BEAMS // 2
         for side in range(2):
             lanes = slice(side * width, (side + 1) * width)
@@ -371,19 +393,19 @@
     blocks = LANES // 16
     per_block = local // blocks
 
-    def add_source(u, later, steering_on):
+    def add_source(u, later, steering_on, finish=None):
         slot = lax.rem(u, 2)
         gain_ref = gains if later else lent
         source = owner(u) if later else owner(u) - side * m
         at = pl.multiple_of(source * LANES, LANES)
-        if steering_on:
-            place(owner(u + 1))
 
         def body(block, carry):
             if steering_on:
                 steer(block, 1 - slot, u + 1)
             for c in range(per_block):
                 add_channel(block * per_block + c, u, slot, gain_ref, at)
+                if finish is not None:
+                    finish(block * per_block + c)
             return carry
 
         lax.fori_loop(0, blocks, body, 0, unroll=1 if steering_on else 4)
@@ -392,8 +414,13 @@
         steer(block, 0, 0)
         return carry
 
-    place(me)
+    def place_all(u, carry):
+        place(u)
+        return carry
+
+    place(0)
     lax.fori_loop(0, blocks, first_steer, 0)
+    lax.fori_loop(1, m, place_all, 0)
     lend.wait()
     add_source(0, False, True)
 
@@ -402,15 +429,14 @@
         add_source(u, False, True)
         return carry
 
-    lax.fori_loop(1, m, for_twin, 0)
-
-    def hand_over(c, carry):
+    def hand_over(c):
         leaving[c] = sums[c].astype(bf16)
         partial(c).start()
         sums[c] = jnp.zeros((2 * TIME, BEAMS), f32)
-        return carry
-
-    lax.fori_loop(0, local, hand_over, 0)
+
+    lax.fori_loop(1, m - 1, for_twin, 0)
+    turned(m - 1).wait_recv()
+    add_source(m - 1, False, True, hand_over)
     add_source(m, True, True)
 
     def for_self(u, carry):
@@ -420,15 +446,13 @@
 
     lax.fori_loop(m + 1, n - 1, for_self, 0)
     turned(n - 1).wait_recv()
-    add_source(n - 1, True, False)
-
-    def detect(c, carry):
+
+    def detect(c):
         partial(c).wait()
         total = sums[c] + landing[c].astype(f32)
         power[c] = total[:TIME] * total[:TIME] + total[TIME:] * total[TIME:]
-        return carry
-
-    lax.fori_loop(0, local, detect, 0)
+
+    add_source(n - 1, True, False, detect)
     flat = power[...].reshape(local * TIME, BEAMS)
     high = flat.astype(bf16)
     low = (flat - high.astype(f32)).astype(bf16)
@@ -496,11 +520,12 @@
         out_specs=(vmem, vmem),
         scratch_shapes=[
             pltpu.VMEM((2 * CH, FFTLEN), bf16),
+            pltpu.VMEM((TIME // 2, 2 * LANES, FFTLEN), bf16),
             pltpu.VMEM((TIME * 2 * CH, LANES), f32),
             pltpu.VMEM((n, rows, TIME, LANES), bf16),
             pltpu.VMEM((n, rows, TIME, LANES), bf16),
             pltpu.VMEM((48, INPUTS), bf16),
-            pltpu.VMEM((LANES, LANES), f32),
+            pltpu.VMEM((n // 2, LANES, LANES), f32),
             pltpu.VMEM((2, local, 2 * LANES, BEAMS), bf16),
             pltpu.VMEM((local, 2 * TIME, BEAMS), f32),
             pltpu.VMEM((half, 2 * trials, 2 * CH), bf16),

time: 113 us -> 109 us (0.965)
  Pallas kernels: 107 us -> 104 us
    pallas_call x1, Pallas kernels: 107 us -> 104 us  [crate_device(): pl.pallas_call(functools.partial(crate_kernel, n), out_shape=(jax.ShapeDt...]
where the time goes in v4:
time: 109 us
  Pallas kernels  104 us (95%)
  local copies, waits for them, and re-layouts  3.96 us (4%)
    pallas_call x1, Pallas kernels, crate_device(): pl.pallas_call(functools.partial(crate_kernel, n), out_shape=(jax.ShapeDt...  104 us
    unnamed x2, local copies, waits for them, and re-layouts  3.96 us

profile of v4, /device:TPU:0, one launch (start us, length us, event | category | flops | bytes accessed | tf_op | source)
XLA Modules:
  0.0 108.8 jit_solution(5785857798024807241)
XLA Ops:
  0.6 104.2 %shard_map.113 = (f32[16,32,512]{2,1,0:T(8,128)}, f32[16,32,64]{2,1,0:T(8,128)}) custom-call(bf16[128,17920]{1,0:T(8,128)(2,1)} %volts.1, f32[4,512]{1,0:T(4,128)} %constant.6.clone.window, f32[512,512]{1,0:T(8,128)} %constant.7.clone.dft, f32[16,2,2048]{2,1,0:T(2,128)} %gains.1, f32[3,2048]{1,0:T(4,128)} %positions.1, f32[3,512]{1,0:T(4,128)} %directions.1, ...), custom_call_target="tpu_custom_call" | custom-call | tf_op jit(solution)/shard_map/pallas_call | solution.py:513
  104.8 2.3 %copy.14 = f32[16,512,32]{1,2,0:T(8,128)} copy(f32[16,512,32]{1,2,0:T(8,128)} %bitcast.4) | data formatting | bytes 2097152
  107.1 1.7 %copy.15 = f32[64,16,32]{0,2,1:T(8,128)} copy(f32[64,16,32]{0,2,1:T(8,128)} %bitcast.5) | data formatting | bytes 262144

commit v5 on v4

--- a/solution.py
+++ b/solution.py
@@ -216,11 +216,21 @@
     def peer(step):
         return lax.rem(me + step, n)
 
+    w = m // 2
+    layer = place_in // w
+    seat = lax.rem(place_in, w)
+
+    def layer_of(u):
+        return lax.rem(layer + u % m // w, 2) * w
+
+    def spot(u):
+        return layer_of(u) + lax.rem(seat + u, w)
+
     def near(u):
-        return side * m + lax.rem(place_in + u, m)
+        return side * m + spot(u)
 
     def owner(u):
-        return side * m + lax.rem(place_in - u + 2 * m, m)
+        return side * m + layer_of(u) + lax.rem(seat - u + 2 * m, w)
 
     def channel_side(u):
         return side + (1 - u // m) * (1 - 2 * side)
@@ -265,7 +275,7 @@
         lax.fori_loop(0, TIME // 2, body, 0, unroll=2)
 
     def pack(u):
-        first = (channel_side(u) * m + lax.rem(place_in + u, m)) * rows
+        first = (channel_side(u) * m + spot(u)) * rows
         for row in range(rows):
             sent[u, row] = frames[pl.ds(first + row, TIME, stride=2 * CH), :].astype(bf16)
 
@@ -307,13 +317,18 @@
         turned(u).start()
         return carry
 
-    lax.fori_loop(1, m, send, 0)
+    lax.fori_loop(w, m, send, 0)
+    lax.fori_loop(1, w, send, 0)
     pack(0)
     own_first = pltpu.make_async_copy(sent.at[0], held.at[0], own_sem.at[0])
     own_first.start()
     channelize(side, False)
-    lax.fori_loop(m + 1, n, send, 0)
-    pack(m)
+
+    def prepare(u, carry):
+        pack(u)
+        return carry
+
+    lax.fori_loop(m, n, prepare, 0)
     own_later = pltpu.make_async_copy(sent.at[m], held.at[m], own_sem.at[1])
     own_later.start()
 
@@ -426,6 +441,7 @@
 
     def for_twin(u, carry):
         turned(u).wait_recv()
+        turned(m + u).start()
         add_source(u, False, True)
         return carry
 
@@ -436,6 +452,7 @@
 
     lax.fori_loop(1, m - 1, for_twin, 0)
     turned(m - 1).wait_recv()
+    turned(n - 1).start()
     add_source(m - 1, False, True, hand_over)
     add_source(m, True, True)
 
@@ -566,6 +583,6 @@
     in_specs = (P(("groups", "crate"), None), P("crate", None, None), P(), P(), P(), P(), P())
     out_specs = (P(("groups", "crate"), None, None), P(("groups", "crate"), None, None))
     n = mesh.shape["crate"]
-    fits = n % 2 == 0 and INPUTS // n == LANES and (CH // n) % 16 == 0 and (TRIALS // n) % 16 == 0
+    fits = n % 4 == 0 and INPUTS // n == LANES and (CH // n) % 16 == 0 and (TRIALS // n) % 16 == 0
     body = functools.partial(crate_device, n) if fits else plain_device
     return jax.shard_map(body, mesh=mesh, in_specs=in_specs, out_specs=out_specs, check_vma=False)

time: 109 us -> 109 us (level)
  no operation moved by 1% of the time
where the time goes in v5:
time: 109 us
  Pallas kernels  105 us (96%)
  local copies, waits for them, and re-layouts  3.96 us (4%)
    pallas_call x1, Pallas kernels, crate_device(): pl.pallas_call(functools.partial(crate_kernel, n), out_shape=(jax.ShapeDt...  105 us
    unnamed x2, local copies, waits for them, and re-layouts  3.96 us

profile of v5, /device:TPU:0, one launch (start us, length us, event | category | flops | bytes accessed | tf_op | source)
XLA Modules:
  0.0 109.3 jit_solution(4628307312673280373)
XLA Ops:
  0.6 104.7 %shard_map.113 = (f32[16,32,512]{2,1,0:T(8,128)}, f32[16,32,64]{2,1,0:T(8,128)}) custom-call(bf16[128,17920]{1,0:T(8,128)(2,1)} %volts.1, f32[4,512]{1,0:T(4,128)} %constant.6.clone.window, f32[512,512]{1,0:T(8,128)} %constant.7.clone.dft, f32[16,2,2048]{2,1,0:T(2,128)} %gains.1, f32[3,2048]{1,0:T(4,128)} %positions.1, f32[3,512]{1,0:T(4,128)} %directions.1, ...), custom_call_target="tpu_custom_call" | custom-call | tf_op jit(solution)/shard_map/pallas_call | solution.py:530
  105.3 2.3 %copy.14 = f32[16,512,32]{1,2,0:T(8,128)} copy(f32[16,512,32]{1,2,0:T(8,128)} %bitcast.4) | data formatting | bytes 2097152
  107.6 1.7 %copy.15 = f32[64,16,32]{0,2,1:T(8,128)} copy(f32[64,16,32]{0,2,1:T(8,128)} %bitcast.5) | data formatting | bytes 262144
